TPU v7x, 128 devices: a whole 4x4x4 slice. The times are simulated.
128 devices in a mesh: row: 16 (over z, x), col: 8 (over y, core).
Axes of the slice: x: 4, y: 4, z: 4, core: 2. Of those that a mesh axis runs over, the one named last changes fastest.
Arguments:
- resid: bfloat16 [8192, 6144], P('row', 'col'), may hold values from -30 to 30
- attn: bfloat16 [8192, 6144], P('row', 'col'), may hold values from -7 to 7
- attn_tangent: bfloat16 [8192, 6144], P('row', 'col'), may hold values from -7 to 7
- probe: int32 [8192, 6144], P('row', 'col'), may hold values from -1 to 1, as said below
- norm_gain: float32 [6144], P('col'), may hold values from 0.1 to 1.9
- gate_weight: bfloat16 [6144, 8192], P('row', 'col'), may hold values from -0.078125 to 0.078125
- up_weight: bfloat16 [6144, 8192], P('row', 'col'), may hold values from -0.078125 to 0.078125
Outputs:
- state: bfloat16 [8192, 6144], P('row', 'col')
- state_tangent: bfloat16 [8192, 6144], P('row', 'col')
- hidden: bfloat16 [8192, 8192], P('row', 'col')
- hidden_tangent: bfloat16 [8192, 8192], P('row', 'col')
Inputs may be any that keep to these rules, and one draw needn't show every extreme that they name: `probe`: each entry is -1 or +1.
All inputs are finite; a program needn't handle non-finite values.
Results may differ from a plain program's by a relative error of at most 0.0078.
Values may be sent and summed in bfloat16 or wider, within the bound.
A program may use at most 512 MiB of HBM per device.

v0:
```python
import jax
import jax.numpy as jnp
from jax import lax
from jax.sharding import PartitionSpec as P

D = 6144


EPS = 1e-06


def local(resid, attn, attn_tangent, probe, norm_gain, gate_weight, up_weight):
    tok_rows = resid.shape[0]
    hid_cols = gate_weight.shape[1]
    state = (resid.astype(jnp.float32) + attn.astype(jnp.float32)).astype(jnp.bfloat16)
    state_tangent = (probe.astype(jnp.float32) + attn_tangent.astype(jnp.float32)).astype(
        jnp.bfloat16
    )
    yval = state.astype(jnp.float32)
    tval = state_tangent.astype(jnp.float32)
    squares, crossed = lax.psum((jnp.sum(yval * yval, axis=1), jnp.sum(yval * tval, axis=1)), "col")
    rate = lax.rsqrt(squares / D + EPS)[:, None]
    cross = (crossed / D)[:, None]
    normed = (yval * rate * norm_gain).astype(jnp.bfloat16)
    normed_tan = (norm_gain * rate * (tval - yval * (cross * rate * rate))).astype(jnp.bfloat16)
    stacked = jnp.stack([normed, normed_tan], axis=1)
    wide_normed = lax.all_gather(stacked, "col", axis=2, tiled=True)
    flat = wide_normed.reshape(2 * tok_rows, -1)
    gate = jnp.dot(
        flat,
        lax.all_gather(gate_weight, "row", axis=0, tiled=True),
        preferred_element_type=jnp.float32,
    )
    upper = jnp.dot(
        flat,
        lax.all_gather(up_weight, "row", axis=0, tiled=True),
        preferred_element_type=jnp.float32,
    )
    gate = gate.reshape(tok_rows, 2, hid_cols)
    upper = upper.reshape(tok_rows, 2, hid_cols)
    gate_val = gate[:, 0]
    upper_val = upper[:, 0]
    sig = jax.nn.sigmoid(gate_val)
    active = gate_val * sig
    hidden = (active * upper_val).astype(jnp.bfloat16)
    slope = sig * (1.0 + gate_val * (1.0 - sig))
    hidden_tangent = (slope * gate[:, 1] * upper_val + active * upper[:, 1]).astype(jnp.bfloat16)
    return (state, state_tangent, hidden, hidden_tangent)


def solution(mesh):
    in_specs = (
        P("row", "col"),
        P("row", "col"),
        P("row", "col"),
        P("row", "col"),
        P("col"),
        P("row", "col"),
        P("row", "col"),
    )
    out_specs = (P("row", "col"), P("row", "col"), P("row", "col"), P("row", "col"))
    return jax.shard_map(local, mesh=mesh, in_specs=in_specs, out_specs=out_specs, check_vma=False)
```

profile of v0, /device:TPU:1, one launch (start us, length us, event | category | flops | bytes accessed | tf_op | source)
XLA Modules:
  0.0 305.8 jit_solution(16574311974204449800)
XLA Ops:
  7.2 0.0 all-gather.4.cloned.1.call-start
  7.2 0.0 copy-start.3
  7.2 2.7 fusion.12
  9.9 0.0 copy-start.1
  10.0 0.0 copy-start.2
  10.0 13.5 %all-reduce = (f32[512]{0:T(512)S(1)}, f32[512]{0:T(512)S(1)}) all-reduce(f32[512]{0:T(512)S(1)} %get-tuple-element.5, f32[512]{0:T(512)S(1)} %get-tuple-element.4), channel_id=1, replica_groups=mesh['row'=16,'col'=8] {'col'}, use_global_device_ids=true, to_apply=%region_3.0 | all-reduce | flops 1024 | bytes 8192 | tf_op jit(solution)/shard_map/psum | solution.py:21
  23.4 0.0 copy-done.3
  23.4 0.6 fusion.16
  24.0 1.3 pad_maximum_fusion
  25.3 0.0 copy-done.1
  25.3 0.0 copy-done.2
  25.3 0.0 all-gather.4.cloned.1.call-update
  25.3 0.0 all-gather.8.cloned.1.call-start
  25.4 0.7 all-gather.8.cloned.1.call-update
  26.1 0.0 all-gather.6.cloned.1.call-start
  26.1 0.7 all-gather.6.cloned.1.call-update
  26.8 68.4 %all-gather.4.cloned.1.call-done = bf16[512,2,6144]{2,0,1:T(8,128)(2,1)} async-done(((bf16[512,2,768]{2,0,1:T(8,128)(2,1)}), bf16[512,2,6144]{2,0,1:T(8,128)(2,1)}) %all-gather.4.cloned.1.call-update) | async-done | bytes 12582928 | tf_op jit(solution)/shard_map/all_gather | solution.py:27
  95.2 92.3 %all-gather.8.cloned.1.call-done = bf16[6144,1024]{1,0:T(8,128)(2,1)} async-done(((bf16[384,1024]{1,0:T(8,128)(2,1)}), bf16[6144,1024]{1,0:T(8,128)(2,1)}) %all-gather.8.cloned.1.call-update) | async-done | bytes 12582928 | tf_op jit(solution)/shard_map/all_gather | solution.py:36
  187.5 19.0 %fusion = f32[512,2,1024]{2,0,1:T(8,128)} fusion(bf16[512,2,6144]{2,0,1:T(8,128)(2,1)} %all-gather.4.cloned.1.call-done, bf16[6144,1024]{1,0:T(8,128)(2,1)} %all-gather.8.cloned.1.call-done), kind=kOutput, calls=%fused_computation | convolution fusion | flops 12884901888 | bytes 29360128 | tf_op jit(solution)/shard_map/dot_general | solution.py:34
  206.5 72.9 %all-gather.6.cloned.1.call-done = bf16[6144,1024]{1,0:T(8,128)(2,1)} async-done(((bf16[384,1024]{1,0:T(8,128)(2,1)}), bf16[6144,1024]{1,0:T(8,128)(2,1)}) %all-gather.6.cloned.1.call-update) | async-done | bytes 12582928 | tf_op jit(solution)/shard_map/all_gather | solution.py:31
  279.4 0.0 copy-start
  279.4 17.3 %fusion.2 = f32[512,2,1024]{2,0,1:T(8,128)S(1)} fusion(bf16[512,2,6144]{2,0,1:T(8,128)(2,1)} %all-gather.4.cloned.1.call-done, bf16[6144,1024]{1,0:T(8,128)(2,1)} %all-gather.6.cloned.1.call-done), kind=kOutput, calls=%fused_computation.2 | convolution fusion | flops 12884901888 | bytes 29360128 | tf_op jit(solution)/shard_map/dot_general | solution.py:29
  296.7 0.0 copy-done
  296.7 2.5 fusion.6
  (1 shorter events, 0.0 us)
Async XLA Ops:
  7.2 88.0 %all-gather.4.cloned.1.call-start = ((), (), s32[]{:S(2)}) async-start(), calls=%async_computation | async-start | bytes 14155776 | tf_op jit(solution)/shard_map/all_gather | solution.py:27
  7.2 16.2 %copy-start.3 = (f32[768]{0:T(1024)S(1)}, f32[768]{0:T(1024)}, u32[]{:S(2)}) copy-start(f32[768]{0:T(1024)} %param.11) | copy-start | bytes 9220
  9.9 15.3 %copy-start.1 = (bf16[512,768]{1,0:T(8,128)(2,1)}, bf16[512,768]{1,0:T(8,128)(2,1)S(1)}, u32[]{:S(2)}) copy-start(bf16[512,768]{1,0:T(8,128)(2,1)S(1)} %get-tuple-element.8) | copy-start | bytes 2359300
  10.0 15.3 %copy-start.2 = (bf16[512,768]{1,0:T(8,128)(2,1)}, bf16[512,768]{1,0:T(8,128)(2,1)S(1)}, u32[]{:S(2)}) copy-start(bf16[512,768]{1,0:T(8,128)(2,1)S(1)} %get-tuple-element.9) | copy-start | bytes 2359300
  25.3 162.2 %all-gather.8.cloned.1.call-start = ((), (), s32[]{:S(2)}) async-start(), calls=%async_computation.2 | async-start | bytes 13369344 | tf_op jit(solution)/shard_map/all_gather | solution.py:36
  26.1 253.3 %all-gather.6.cloned.1.call-start = ((), (), s32[]{:S(2)}) async-start(), calls=%async_computation.1 | async-start | bytes 13369344 | tf_op jit(solution)/shard_map/all_gather | solution.py:31
  279.4 17.3 %copy-start = (f32[512,2,1024]{2,0,1:T(8,128)S(1)}, f32[512,2,1024]{2,0,1:T(8,128)}, u32[]{:S(2)}) copy-start(f32[512,2,1024]{2,0,1:T(8,128)} %fusion) | copy-start | bytes 12582916
Sparse Core Ops, SparseCore 0:
  25.4 69.7 all-gather.3
  97.3 90.1 all-gather.7
  189.6 89.7 all-gather.5
where the time goes:
time: 306 us
  waiting for transfers between devices  235 us (77%)
  matrix products  36.3 us (12%)
  between operations  13.8 us (5%)
  blocking collectives  13.5 us (4%)
  other arithmetic  7.1 us (2%)
    all_gather x1, waiting for transfers between devices, local(): lax.all_gather(up_weight, 'row', axis=0, tiled=True)  92.3 us
    all_gather x1, waiting for transfers between devices, local(): lax.all_gather(gate_weight, 'row', axis=0, tiled=True)  72.9 us
    all_gather x1, waiting for transfers between devices, local(): wide_normed = lax.all_gather(stacked, 'col', axis=2, tiled=True)  68.4 us
    dot_general x1, matrix products, local(): jnp.dot(flat, lax.all_gather(up_weight, 'row', axis=0, tiled=True), prefe...  19 us
    dot_general x1, matrix products, local(): jnp.dot(flat, lax.all_gather(gate_weight, 'row', axis=0, tiled=True), pre...  17.3 us
    psum x1, blocking collectives, local(): lax.psum((jnp.sum(yval * yval, axis=1), jnp.sum(yval * tval, axis=1)), 'c...  13.5 us
  transfers between devices with their start and end apart: 3, of which 3 were waited for; matrix products, arithmetic and copies ran while one was open for 6% of the time, Pallas kernels for 0%

commit v1 on v0

v1 whole, which is shorter than its diff:
```python
import functools

import jax
import jax.numpy as jnp
from jax import lax
from jax.experimental import pallas as pl
from jax.experimental.pallas import tpu as pltpu
from jax.sharding import PartitionSpec as P

MESH = pl.DeviceIdType.MESH
EPS = 1e-06
D = 6144
TOK = 512
HALF = TOK // 2
FEAT = 768
DEPTH = 384
HID = 1024
UNIT = 128
CHUNKS = HID // UNIT
MM_TOK = 256
NORM_TOK = 16

FROM_PREV, FROM_NEXT, OPP_LO, OPP_HI = 0, 1, 2, 3
LINE_PREV, LINE_NEXT, LINE_LO, LINE_HI = 4, 8, 12, 16


def body(
    resid, attn, attn_tan, probe, gain, gate_w, up_w,
    state_out, state_tan_out, hid_out, hid_tan_out,
    weights, acts, raw, spare, gains, in_res, in_att, in_tan, in_pro,
    w_send, w_recv, a_send, a_recv, loc,
):
    row, col = lax.axis_index("row"), lax.axis_index("col")
    z, x, y, core = row // 4, row % 4, col // 2, col % 2

    def near(pos, axis, step):
        if axis == "z":
            return {"row": ((z + step) % 4) * 4 + x, "col": col}
        if axis == "x":
            return {"row": z * 4 + (x + step) % 4, "col": col}
        return {"row": row, "col": ((y + step) % 4) * 2 + core}

    to = {(a, s): near(None, a, s) for a in "xyz" for s in (1, -1)}
    sibling = {"row": row, "col": y * 2 + 1 - core}

    loads = [
        pltpu.make_async_copy(src, dst, loc.at[n])
        for n, (src, dst) in enumerate(
            ((resid, in_res), (attn, in_att), (attn_tan, in_tan), (probe, in_pro))
        )
    ]

    def stage(j, n):
        cols = pl.ds(pl.multiple_of(j * UNIT, UNIT), UNIT)
        mine = weights.at[j, z, x]
        return (
            pltpu.make_async_copy(gate_w.at[:, cols], mine.at[:, pl.ds(0, UNIT)], loc.at[4 + 2 * n]),
            pltpu.make_async_copy(up_w.at[:, cols], mine.at[:, pl.ds(UNIT, UNIT)], loc.at[5 + 2 * n]),
        )

    staged = [stage(j, j) for j in range(CHUNKS)]
    for pair in staged:
        for copy in pair:
            copy.start()
    for copy in loads:
        copy.start()

    barrier = pltpu.get_barrier_semaphore()
    for other in (*to.values(), sibling):
        pl.semaphore_signal(barrier, inc=1, device_id=other, device_id_type=MESH)
    pl.semaphore_wait(barrier, 7)

    def axes(kind):
        return ("x", "z") if kind == 0 else ("z", "x")

    def spot(kind, j, first, second):
        if kind == 0:
            return weights.at[j, (z + second) % 4, (x + first) % 4]
        return weights.at[j, (z + first) % 4, (x + second) % 4]

    def wsend(j, ref, sem, msg, axis, step):
        return pltpu.make_async_remote_copy(
            src_ref=ref, dst_ref=ref, send_sem=w_send.at[j, sem], recv_sem=w_recv.at[j, msg],
            device_id=to[axis, step], device_id_type=MESH,
        )

    def wwait(j, ref, msg):
        pltpu.make_async_copy(ref, ref, w_recv.at[j, msg]).wait()

    lo, hi = pl.ds(0, DEPTH // 2), pl.ds(DEPTH // 2, DEPTH // 2)

    def own(kind, j):
        a, b = axes(kind)
        mine = spot(kind, j, 0, 0)
        wsend(j, mine, 0, FROM_PREV, a, 1).start()
        wsend(j, mine, 1, FROM_NEXT, a, -1).start()
        wsend(j, mine, 2, LINE_PREV, b, 1).start()
        wsend(j, mine, 3, LINE_NEXT, b, -1).start()

    def first_near(kind, j):
        a, b = axes(kind)
        prev, nxt = spot(kind, j, -1, 0), spot(kind, j, 1, 0)
        wwait(j, prev, FROM_PREV)
        wsend(j, prev.at[lo], 4, OPP_LO, a, 1).start()
        wsend(j, prev, 5, LINE_PREV + 1, b, 1).start()
        wsend(j, prev, 6, LINE_NEXT + 1, b, -1).start()
        wwait(j, nxt, FROM_NEXT)
        wsend(j, nxt.at[hi], 7, OPP_HI, a, -1).start()
        wsend(j, nxt, 8, LINE_PREV + 2, b, 1).start()
        wsend(j, nxt, 9, LINE_NEXT + 2, b, -1).start()

    def first_far(kind, j):
        _, b = axes(kind)
        opp = spot(kind, j, 2, 0)
        wwait(j, opp.at[lo], OPP_LO)
        wwait(j, opp.at[hi], OPP_HI)
        wsend(j, opp, 10, LINE_PREV + 3, b, 1).start()
        wsend(j, opp, 11, LINE_NEXT + 3, b, -1).start()

    firsts = (0, -1, 1, 2)

    def second_near(kind, j):
        _, b = axes(kind)
        for q, first in enumerate(firsts):
            prev, nxt = spot(kind, j, first, -1), spot(kind, j, first, 1)
            wwait(j, prev, LINE_PREV + q)
            wsend(j, prev.at[lo], 12 + q, LINE_LO + q, b, 1).start()
            wwait(j, nxt, LINE_NEXT + q)
            wsend(j, nxt.at[hi], 16 + q, LINE_HI + q, b, -1).start()

    def second_far(kind, j):
        for q, first in enumerate(firsts):
            opp = spot(kind, j, first, 2)
            wwait(j, opp.at[lo], LINE_LO + q)
            wwait(j, opp.at[hi], LINE_HI + q)

    def drain(kind, j):
        _, b = axes(kind)
        whole, half = spot(kind, j, 0, 0), spot(kind, j, 0, 0).at[lo]
        for sem in range(20):
            ref = half if sem in (4, 7) or sem >= 12 else whole
            pltpu.make_async_copy(ref, ref, w_send.at[j, sem]).wait()

    for j in range(CHUNKS):
        for copy in staged[j]:
            copy.wait()
        if j < 3:
            own(j % 2, j)

    for copy in loads:
        copy.wait()
    gains[y, core] = jnp.broadcast_to(gain[...], (8, FEAT))

    def add(rows, target):
        def step(n, _):
            here = pl.ds(pl.multiple_of(rows + n * 32, 32), 32)
            there = pl.ds(pl.multiple_of(n * 32, 32), 32)
            target[0, there, :] = (
                in_res[here, :].astype(jnp.float32) + in_att[here, :].astype(jnp.float32)
            ).astype(jnp.bfloat16)
            target[1, there, :] = (
                in_pro[here, :].astype(jnp.float32) + in_tan[here, :].astype(jnp.float32)
            ).astype(jnp.bfloat16)
            return 0

        lax.fori_loop(0, HALF // 32, step, 0)

    def asend(ref, dst, sem, msg, device):
        return pltpu.make_async_remote_copy(
            src_ref=ref, dst_ref=dst, send_sem=a_send.at[sem], recv_sem=a_recv.at[msg],
            device_id=device, device_id_type=MESH,
        )

    def await_(ref, sem):
        pltpu.make_async_copy(ref, ref, sem).wait()

    add((1 - core) * HALF, spare)
    raw_mine, raw_sib = raw.at[y, core], raw.at[y, 1 - core]
    gain_mine, gain_sib = gains.at[y, core], gains.at[y, 1 - core]
    asend(spare, raw_mine, 0, 0, sibling).start()
    asend(gain_mine, gain_mine, 1, 1, sibling).start()
    add(core * HALF, raw_mine)
    asend(raw_mine, raw_mine, 2, 2, to["y", 1]).start()
    asend(raw_mine, raw_mine, 3, 3, to["y", -1]).start()
    stores = []
    for n, (half, src) in enumerate((((1 - core), spare), (core, raw_mine))):
        rows = pl.ds(pl.multiple_of(half * HALF, HALF), HALF)
        stores.append(pltpu.make_async_copy(src.at[0], state_out.at[rows], loc.at[20 + 2 * n]))
        stores.append(pltpu.make_async_copy(src.at[1], state_tan_out.at[rows], loc.at[21 + 2 * n]))
    for copy in stores:
        copy.start()
    await_(raw_sib, a_recv.at[0])
    await_(gain_sib, a_recv.at[1])
    asend(raw_sib, raw_sib, 4, 4, to["y", 1]).start()
    asend(raw_sib, raw_sib, 5, 5, to["y", -1]).start()
    gain_row = gains.at[y]
    asend(gain_row, gain_row, 6, 6, to["y", 1]).start()
    asend(gain_row, gain_row, 7, 7, to["y", -1]).start()

    prev_y, next_y, opp_y = (y + 3) % 4, (y + 1) % 4, (y + 2) % 4

    def acts_near():
        await_(raw.at[prev_y, core], a_recv.at[2])
        asend(raw.at[prev_y, core], raw.at[prev_y, core], 8, 8, to["y", 1]).start()
        await_(raw.at[next_y, core], a_recv.at[3])
        await_(raw.at[prev_y, 1 - core], a_recv.at[4])
        await_(raw.at[next_y, 1 - core], a_recv.at[5])
        asend(raw.at[next_y, 1 - core], raw.at[next_y, 1 - core], 9, 9, to["y", -1]).start()
        await_(gains.at[prev_y], a_recv.at[6])
        await_(gains.at[next_y], a_recv.at[7])
        asend(gains.at[prev_y], gains.at[prev_y], 10, 10, to["y", 1]).start()

    def acts_far():
        await_(raw.at[opp_y, core], a_recv.at[8])
        await_(raw.at[opp_y, 1 - core], a_recv.at[9])
        await_(gains.at[opp_y], a_recv.at[10])

        def step(n, _):
            rows = pl.ds(pl.multiple_of(n * NORM_TOK, NORM_TOK), NORM_TOK)
            squares = jnp.zeros((NORM_TOK, FEAT), jnp.float32)
            crossed = jnp.zeros((NORM_TOK, FEAT), jnp.float32)
            for g in range(4):
                for p in range(2):
                    yval = raw[g, p, 0, rows, :].astype(jnp.float32)
                    tval = raw[g, p, 1, rows, :].astype(jnp.float32)
                    squares += yval * yval
                    crossed += yval * tval
            rate = lax.rsqrt(jnp.sum(squares, axis=1, keepdims=True) / D + EPS)
            cross = jnp.sum(crossed, axis=1, keepdims=True) / D
            pull = cross * rate * rate
            to_rows = pl.ds(pl.multiple_of(core * HALF + n * NORM_TOK, NORM_TOK), NORM_TOK)
            for g in range(4):
                for p in range(2):
                    yval = raw[g, p, 0, rows, :].astype(jnp.float32)
                    tval = raw[g, p, 1, rows, :].astype(jnp.float32)
                    scale = gains[g, p, 0:1, :]
                    cols = pl.ds((2 * g + p) * FEAT, FEAT)
                    acts[0, to_rows, cols] = (yval * rate * scale).astype(jnp.bfloat16)
                    acts[1, to_rows, cols] = (scale * rate * (tval - yval * pull)).astype(jnp.bfloat16)
            return 0

        lax.fori_loop(0, HALF // NORM_TOK, step, 0)
        done = acts.at[:, pl.ds(pl.multiple_of(core * HALF, HALF), HALF), :]
        asend(done, done, 11, 11, sibling).start()

    def acts_whole():
        other = acts.at[:, pl.ds(pl.multiple_of((1 - core) * HALF, HALF), HALF), :]
        await_(other, a_recv.at[11])

    def multiply(j):
        def step(n, _):
            rows = pl.ds(pl.multiple_of(n * MM_TOK, MM_TOK), MM_TOK)
            lhs = jnp.concatenate([acts[0, rows, :], acts[1, rows, :]], axis=0)
            out = jnp.dot(lhs, weights[j].reshape(D, 2 * UNIT), preferred_element_type=jnp.float32)
            gate, upper = out[:MM_TOK, :UNIT], out[:MM_TOK, UNIT:]
            gate_t, upper_t = out[MM_TOK:, :UNIT], out[MM_TOK:, UNIT:]
            sig = jax.nn.sigmoid(gate)
            active = gate * sig
            slope = sig * (1.0 + gate * (1.0 - sig))
            cols = pl.ds(pl.multiple_of(j * UNIT, UNIT), UNIT)
            hid_out[rows, cols] = (active * upper).astype(jnp.bfloat16)
            hid_tan_out[rows, cols] = (slope * gate_t * upper + active * upper_t).astype(jnp.bfloat16)
            return 0

        lax.fori_loop(0, TOK // MM_TOK, step, 0)

    def slot(t, kind):
        pl.when(t + 3 < CHUNKS)(lambda: own(1 - kind, t + 3))
        pl.when(t < CHUNKS)(lambda: first_near(kind, t))
        pl.when((t >= 1) & (t - 1 < CHUNKS))(lambda: second_near(1 - kind, t - 1))
        pl.when(t < CHUNKS)(lambda: first_far(kind, t))
        pl.when((t >= 2) & (t - 2 < CHUNKS))(lambda: second_far(kind, t - 2))
        if kind == 1:
            pl.when(t == 3)(acts_near)
            pl.when(t == 5)(acts_whole)
        else:
            pl.when(t == 4)(acts_far)
        begin = jnp.where(t < 5, 0, jnp.minimum(2 * (t - 5), t - 2))
        end = jnp.where(t < 5, 0, jnp.minimum(2 * (t - 4), t - 1))

        def item(j, _):
            multiply(j)
            return 0

        lax.fori_loop(begin, end, item, 0)

    def pair(n, _):
        slot(2 * n, 0)
        slot(2 * n + 1, 1)
        return 0

    lax.fori_loop(0, (CHUNKS + 2) // 2, pair, 0)

    def finish(n, _):
        drain(0, 2 * n)
        drain(1, 2 * n + 1)
        return 0

    lax.fori_loop(0, CHUNKS // 2, finish, 0)
    done = acts.at[:, pl.ds(pl.multiple_of(core * HALF, HALF), HALF), :]
    for sem, ref in (
        (0, spare), (1, gain_mine), (2, raw_mine), (3, raw_mine), (4, raw_sib), (5, raw_sib),
        (6, gain_row), (7, gain_row), (8, raw_mine), (9, raw_mine), (10, gain_row), (11, done),
    ):
        await_(ref, a_send.at[sem])
    for copy in stores:
        copy.wait()


def local(resid, attn, attn_tangent, probe, norm_gain, gate_weight, up_weight):
    hbm, vmem = pl.BlockSpec(memory_space=pl.ANY), pl.BlockSpec(memory_space=pltpu.VMEM)
    bf16, f32 = jnp.bfloat16, jnp.float32
    return pl.pallas_call(
        body,
        name="block",
        out_shape=(
            jax.ShapeDtypeStruct((TOK, FEAT), bf16),
            jax.ShapeDtypeStruct((TOK, FEAT), bf16),
            jax.ShapeDtypeStruct((TOK, HID), bf16),
            jax.ShapeDtypeStruct((TOK, HID), bf16),
        ),
        in_specs=[hbm, hbm, hbm, hbm, vmem, hbm, hbm],
        out_specs=(hbm, hbm, vmem, vmem),
        scratch_shapes=[
            pltpu.VMEM((CHUNKS, 4, 4, DEPTH, 2 * UNIT), bf16),
            pltpu.VMEM((2, TOK, D), bf16),
            pltpu.VMEM((4, 2, 2, HALF, FEAT), bf16),
            pltpu.VMEM((2, HALF, FEAT), bf16),
            pltpu.VMEM((4, 2, 8, FEAT), f32),
            pltpu.VMEM((TOK, FEAT), bf16),
            pltpu.VMEM((TOK, FEAT), bf16),
            pltpu.VMEM((TOK, FEAT), bf16),
            pltpu.VMEM((TOK, FEAT), jnp.int32),
            pltpu.SemaphoreType.DMA((CHUNKS, 20)),
            pltpu.SemaphoreType.DMA((CHUNKS, 20)),
            pltpu.SemaphoreType.DMA((12,)),
            pltpu.SemaphoreType.DMA((12,)),
            pltpu.SemaphoreType.DMA((24,)),
        ],
        compiler_params=pltpu.CompilerParams(
            collective_id=0, has_side_effects=True, vmem_limit_bytes=60 << 20
        ),
    )(resid, attn, attn_tangent, probe, norm_gain.reshape(1, FEAT), gate_weight, up_weight)


def solution(mesh):
    in_specs = (
        P("row", "col"),
        P("row", "col"),
        P("row", "col"),
        P("row", "col"),
        P("col"),
        P("row", "col"),
        P("row", "col"),
    )
    out_specs = (P("row", "col"), P("row", "col"), P("row", "col"), P("row", "col"))
    return jax.shard_map(local, mesh=mesh, in_specs=in_specs, out_specs=out_specs, check_vma=False)
```

time: 306 us -> 166 us (0.54)
  waiting for transfers between devices: 235 us -> 0 us
  Pallas kernels: 0 us -> 159 us
  matrix products: 36.3 us -> 0 us
  blocking collectives: 13.5 us -> 0 us
  between operations: 13.8 us -> 0.66 us
  other arithmetic: 7.1 us -> 0 us
  local copies, waits for them, and re-layouts: 0.02 us -> 6.29 us
    all_gather x3 -> x0, waiting for transfers between devices: 234 us -> none  [the longest x1 92.3 us: local(): lax.all_gather(up_weight, 'row', axis=0, tiled=True)]
    pallas_call x0 -> x1, Pallas kernels: none -> 159 us  [local(): pl.pallas_call(body, name='block', out_shape=(jax.ShapeDtypeStruct((TOK,...]
    dot_general x2 -> x0, matrix products: 36.3 us -> none  [the longest x1 19 us: local(): jnp.dot(flat, lax.all_gather(up_weight, 'row', axis=0, tiled=True), prefe...]
    psum x1 -> x0, blocking collectives: 13.5 us -> none  [local(): lax.psum((jnp.sum(yval * yval, axis=1), jnp.sum(yval * tval, axis=1)), 'c...]
    unnamed x8 -> x10, local copies, waits for them, and re-layouts: 0.02 us -> 5.03 us
  transfers between devices with their start and end apart: 3 -> 0, of which waited for: 3 -> 0; matrix products, arithmetic and copies ran while one was open for 6% -> 0% of each run, Pallas kernels for 0% -> 0%
where the time goes in v1:
time: 166 us
  Pallas kernels  159 us (96%)
  local copies, waits for them, and re-layouts  6.29 us (4%)
    pallas_call x1, Pallas kernels, local(): pl.pallas_call(body, name='block', out_shape=(jax.ShapeDtypeStruct((TOK,...  159 us
    unnamed x10, local copies, waits for them, and re-layouts  5.03 us

profile of v1, /device:TPU:1, one launch (start us, length us, event | category | flops | bytes accessed | tf_op | source)
XLA Modules:
  0.0 165.7 jit_solution(6294157212369861856)
XLA Ops:
  0.6 1.3 reshape.11.gain
  1.9 158.7 %block.1 = (bf16[512,768]{1,0:T(8,128)(2,1)}, bf16[512,768]{1,0:T(8,128)(2,1)}, bf16[512,1024]{1,0:T(8,128)(2,1)}, bf16[512,1024]{1,0:T(8,128)(2,1)}) custom-call(bf16[512,768]{1,0:T(8,128)(2,1)} %resid.1, bf16[512,768]{1,0:T(8,128)(2,1)} %attn.1, bf16[512,768]{1,0:T(8,128)(2,1)} %attn_tan.1, s32[512,768]{1,0:T(8,128)} %probe.1, f32[1,768]{1,0:T(1,128)} %reshape.11.gain, ...), custom_call_target="tpu_custom_call" | custom-call | tf_op jit(solution)/shard_map/block/pallas_call | solution.py:313
  160.6 0.0 copy-start.2
  160.6 0.0 copy-start.1
  160.7 2.2 %copy.15 = bf16[512,768]{1,0:T(8,128)(2,1)} copy(bf16[512,768]{1,0:T(8,128)(2,1)} %get-tuple-element.8) | data formatting | bytes 1572864
  162.9 0.0 copy-done.2
  162.9 0.0 copy-start
  162.9 0.9 copy.16
  163.7 0.0 copy-done.1
  163.7 1.0 copy.17
  164.7 0.0 copy-done
  164.7 1.0 copy.18
Async XLA Ops:
  160.6 2.2 %copy-start.2 = (bf16[512,768]{1,0:T(8,128)(2,1)S(1)}, bf16[512,768]{1,0:T(8,128)(2,1)}, u32[]{:S(2)}) copy-start(bf16[512,768]{1,0:T(8,128)(2,1)} %get-tuple-element.9) | copy-start | bytes 2359300
  160.6 3.1 %copy-start.1 = (bf16[512,1024]{1,0:T(8,128)(2,1)S(1)}, bf16[512,1024]{1,0:T(8,128)(2,1)}, u32[]{:S(2)}) copy-start(bf16[512,1024]{1,0:T(8,128)(2,1)} %get-tuple-element.10) | copy-start | bytes 3145732
  162.9 1.9 %copy-start = (bf16[512,1024]{1,0:T(8,128)(2,1)S(1)}, bf16[512,1024]{1,0:T(8,128)(2,1)}, u32[]{:S(2)}) copy-start(bf16[512,1024]{1,0:T(8,128)(2,1)} %get-tuple-element.11) | copy-start | bytes 3145732

commit v2 on v0

v2 whole, which is shorter than its diff:
```python
import jax
import jax.numpy as jnp
from jax import lax
from jax.experimental import pallas as pl
from jax.experimental.pallas import tpu as pltpu
from jax.sharding import PartitionSpec as P

MESH = pl.DeviceIdType.MESH
EPS = 1e-06
D = 6144
TOK = 512
HALF = TOK // 2
SUB = 64
FEAT = 768
DEPTH = 384
HID = 1024
UNIT = 128
CHUNKS = HID // 2 // UNIT
EARLY = (CHUNKS - 1) * UNIT
STEPS = 8
RAW = 6


def body(
    resid, attn, attn_tan, probe, gain, gate_w, up_w,
    state_out, state_tan_out, hid_out, hid_tan_out,
    weights, others, acts, raw, spare, gains, results, in_res, in_att, in_tan, in_pro,
    w_send, w_recv, y_send, y_recv, n_send, n_recv, c_send, c_recv, a_send, a_recv, loc,
):
    row, col = lax.axis_index("row"), lax.axis_index("col")
    z, x, y, core = row // 4, row % 4, col // 2, col % 2
    parity = x % 2

    def at_x(step):
        return {"row": z * 4 + (x + step + 4) % 4, "col": col}

    def at_z(step):
        return {"row": ((z + step + 4) % 4) * 4 + x, "col": col}

    def at_y(step):
        return {"row": row, "col": ((y + step + 4) % 4) * 2 + core}

    sibling = {"row": row, "col": y * 2 + 1 - core}
    x_to = at_x(2 * core - 1)

    def send(src, dst, send_sem, recv_sem, device):
        pltpu.make_async_remote_copy(
            src_ref=src, dst_ref=dst, send_sem=send_sem, recv_sem=recv_sem,
            device_id=device, device_id_type=MESH,
        ).start()

    def await_(ref, sem):
        pltpu.make_async_copy(ref, ref, sem).wait()

    def stage(j, n, half, target):
        cols = pl.ds(pl.multiple_of(half * (HID // 2) + j * UNIT, UNIT), UNIT)
        return (
            pltpu.make_async_copy(gate_w.at[:, cols], target.at[:, pl.ds(0, UNIT)], loc.at[4 + 2 * n]),
            pltpu.make_async_copy(up_w.at[:, cols], target.at[:, pl.ds(UNIT, UNIT)], loc.at[5 + 2 * n]),
        )

    staged = [
        (stage(j, 2 * j, parity, weights.at[j, z, x]), stage(j, 2 * j + 1, 1 - parity, others.at[j]))
        for j in range(CHUNKS)
    ]
    for pairs in staged:
        for pair in pairs:
            for copy in pair:
                copy.start()
    loads = [
        pltpu.make_async_copy(src, dst, loc.at[n])
        for n, (src, dst) in enumerate(
            ((resid, in_res), (attn, in_att), (attn_tan, in_tan), (probe, in_pro))
        )
    ]
    for copy in loads:
        copy.start()

    barrier = pltpu.get_barrier_semaphore()
    for other in (at_x(1), at_x(-1), at_x(2), at_y(1), at_y(-1), at_z(1), at_z(-1), sibling):
        pl.semaphore_signal(barrier, inc=1, device_id=other, device_id_type=MESH)
    pl.semaphore_wait(barrier, 8)

    lo, hi = pl.ds(0, DEPTH // 2), pl.ds(DEPTH // 2, DEPTH // 2)
    firsts = (0, -1, 1, 2)

    def spot(j, q, step):
        return weights.at[j, (z + step + 4) % 4, (x + firsts[q] + 4) % 4]

    def send_x(j):
        mine = weights.at[j, z, x]
        send(others.at[j], mine, w_send.at[j, 0], w_recv.at[j, 0], at_x(1))
        send(others.at[j], mine, w_send.at[j, 1], w_recv.at[j, 1], at_x(-1))
        send(mine, mine, w_send.at[j, 2], w_recv.at[j, 2], at_x(2))

    def send_z(j, q):
        block = spot(j, q, 0)
        send(block, block, w_send.at[j, 3 + q], w_recv.at[j, 3 + q], at_z(1))
        send(block, block, w_send.at[j, 7 + q], w_recv.at[j, 7 + q], at_z(-1))

    def along_x(j):
        for q in (1, 2, 3):
            await_(spot(j, q, 0), w_recv.at[j, q - 1])
            send_z(j, q)

    def z_near(j):
        for q in range(4):
            prev, nxt = spot(j, q, -1), spot(j, q, 1)
            await_(prev, w_recv.at[j, 3 + q])
            send(prev.at[lo], prev.at[lo], w_send.at[j, 11 + q], w_recv.at[j, 11 + q], at_z(1))
            await_(nxt, w_recv.at[j, 7 + q])
            send(nxt.at[hi], nxt.at[hi], w_send.at[j, 15 + q], w_recv.at[j, 15 + q], at_z(-1))

    def z_far(j):
        for q in range(4):
            opp = spot(j, q, 2)
            await_(opp.at[lo], w_recv.at[j, 11 + q])
            await_(opp.at[hi], w_recv.at[j, 15 + q])

    for j in range(CHUNKS):
        for pair in staged[j]:
            for copy in pair:
                copy.wait()
        if j < 2:
            send_x(j)
        if j < 3:
            send_z(j, 0)

    for copy in loads:
        copy.wait()
    gains[y, core] = jnp.broadcast_to(gain[...], (8, FEAT))

    def add(half, target):
        def step(s, _):
            for n in range(2):
                here = pl.ds(pl.multiple_of(half * HALF + s * SUB + n * 32, 32), 32)
                there = pl.ds(n * 32, 32)
                target[s, 0, there, :] = (
                    in_res[here, :].astype(jnp.float32) + in_att[here, :].astype(jnp.float32)
                ).astype(jnp.bfloat16)
                target[s, 1, there, :] = (
                    in_pro[here, :].astype(jnp.float32) + in_tan[here, :].astype(jnp.float32)
                ).astype(jnp.bfloat16)
            return 0

        lax.fori_loop(0, HALF // SUB, step, 0)

    own_steps = pl.ds(0, 4)
    raw_mine, raw_sib = raw.at[y, own_steps, core], raw.at[y, own_steps, 1 - core]
    gain_mine, gain_sib, gain_row = gains.at[y, core], gains.at[y, 1 - core], gains.at[y]
    add(1 - core, spare)
    send(spare, raw_mine, a_send.at[0], a_recv.at[0], sibling)
    send(gain_mine, gain_mine, a_send.at[1], a_recv.at[1], sibling)
    add(core, raw_mine)
    stores = []
    for n, (half, src) in enumerate((((1 - core), spare), (core, raw_mine))):
        there = pl.ds(half * 4, 4)
        stores.append(pltpu.make_async_copy(src.at[:, 0], state_out.at[there], loc.at[20 + 2 * n]))
        stores.append(pltpu.make_async_copy(src.at[:, 1], state_tan_out.at[there], loc.at[21 + 2 * n]))
    for copy in stores:
        copy.start()

    def send_y(i):
        block = raw.at[y, i]
        send(block, block, y_send.at[i, 0], y_recv.at[i, 0], at_y(1))
        send(block, block, y_send.at[i, 1], y_recv.at[i, 1], at_y(-1))

    await_(raw_sib, a_recv.at[0])
    send_y(0)
    await_(gain_sib, a_recv.at[1])
    send(gain_row, gain_row, a_send.at[2], a_recv.at[2], at_y(1))
    send(gain_row, gain_row, a_send.at[3], a_recv.at[3], at_y(-1))
    send_y(1)
    along_x(0)
    for s in range(2):
        send(raw.at[y, s], raw.at[y, 4 + s], a_send.at[5 + s], a_recv.at[5 + s], x_to)

    prev_y, next_y, opp_y = (y + 3) % 4, (y + 1) % 4, (y + 2) % 4

    def y_near(i):
        prev, nxt = raw.at[prev_y, i], raw.at[next_y, i]
        await_(prev, y_recv.at[i, 0])
        send(prev.at[0], prev.at[0], y_send.at[i, 2], y_recv.at[i, 2], at_y(1))
        await_(nxt, y_recv.at[i, 1])
        send(nxt.at[1], nxt.at[1], y_send.at[i, 3], y_recv.at[i, 3], at_y(-1))

    def gains_near():
        await_(gains.at[prev_y], a_recv.at[2])
        await_(gains.at[next_y], a_recv.at[3])
        send(gains.at[prev_y], gains.at[prev_y], a_send.at[4], a_recv.at[4], at_y(1))

    def gains_far():
        await_(gains.at[opp_y], a_recv.at[4])

    def y_far(i):
        await_(raw.at[opp_y, i, 0], y_recv.at[i, 2])
        await_(raw.at[opp_y, i, 1], y_recv.at[i, 3])

    def norm(i):
        def step(n, _):
            rows = pl.ds(pl.multiple_of(n * 16, 16), 16)
            squares = jnp.zeros((16, FEAT), jnp.float32)
            crossed = jnp.zeros((16, FEAT), jnp.float32)
            for g in range(4):
                for p in range(2):
                    yval = raw[g, i, p, 0, rows, :].astype(jnp.float32)
                    tval = raw[g, i, p, 1, rows, :].astype(jnp.float32)
                    squares += yval * yval
                    crossed += yval * tval
            rate = lax.rsqrt(jnp.sum(squares, axis=1, keepdims=True) / D + EPS)
            cross = jnp.sum(crossed, axis=1, keepdims=True) / D
            pull = cross * rate * rate
            for g in range(4):
                for p in range(2):
                    yval = raw[g, i, p, 0, rows, :].astype(jnp.float32)
                    tval = raw[g, i, p, 1, rows, :].astype(jnp.float32)
                    scale = gains[g, p, 0:1, :]
                    cols = pl.ds((2 * g + p) * FEAT, FEAT)
                    acts[i, 0, core, rows, cols] = (yval * rate * scale).astype(jnp.bfloat16)
                    acts[i, 1, core, rows, cols] = (scale * rate * (tval - yval * pull)).astype(jnp.bfloat16)
            return 0

        lax.fori_loop(0, SUB // 16, step, 0)

    def send_sibling(i):
        done = acts.at[i, :, core]
        send(done, done, n_send.at[i], n_recv.at[i], sibling)

    def await_sibling(i):
        await_(acts.at[i, :, 1 - core], n_recv.at[i])

    def send_normed(i):
        send(acts.at[i, :, core], acts.at[i + 4, :, core], a_send.at[5 + i], a_recv.at[5 + i], x_to)

    def take_normed(i):
        await_(acts.at[i, :, core], a_recv.at[1 + i])
        send_sibling(i)

    def multiply(j, i):
        out = jnp.dot(
            acts[i].reshape(4 * SUB, D), weights[j].reshape(D, 2 * UNIT), preferred_element_type=jnp.float32
        )
        gate, upper = out[: 2 * SUB, :UNIT], out[: 2 * SUB, UNIT:]
        gate_t, upper_t = out[2 * SUB :, :UNIT], out[2 * SUB :, UNIT:]
        sig = jax.nn.sigmoid(gate)
        active = gate * sig
        slope = sig * (1.0 + gate * (1.0 - sig))
        cols = pl.ds(pl.multiple_of(j * UNIT, UNIT), UNIT)
        rows = pl.ds(pl.multiple_of((i % 4) * SUB, SUB), SUB)
        whose = i // 4
        hidden = (active * upper).astype(jnp.bfloat16)
        hidden_tan = (slope * gate_t * upper + active * upper_t).astype(jnp.bfloat16)
        for c in range(2):
            results[whose, 0, c, rows, cols] = hidden[c * SUB : (c + 1) * SUB]
            results[whose, 1, c, rows, cols] = hidden_tan[c * SUB : (c + 1) * SUB]

    def give(part, do):
        begin, width = (0, EARLY) if part == 0 else (EARLY, UNIT)
        here = pl.ds(begin, width)
        there = pl.ds(pl.multiple_of(parity * (HID // 2) + begin, UNIT), width)
        for k, out in enumerate((hid_out, hid_tan_out)):
            for c in range(2):
                n = 4 * part + 2 * k + c
                do(n, results.at[1, k, c, :, here], out.at[pl.ds(c * HALF, HALF), there], at_x(1 - 2 * c))

    def give_start(part):
        give(part, lambda n, src, dst, device: send(src, dst, c_send.at[n], c_recv.at[n], device))

    def keep(part):
        begin, width = (0, EARLY) if part == 0 else (EARLY, UNIT)
        there = pl.ds(pl.multiple_of(parity * (HID // 2) + begin, UNIT), width)
        return [
            pltpu.make_async_copy(
                results.at[0, k, c, :, pl.ds(begin, width)], out.at[pl.ds(c * HALF, HALF), there],
                loc.at[24 + 4 * part + 2 * k + c],
            )
            for k, out in enumerate((hid_out, hid_tan_out))
            for c in range(2)
        ]

    def keep_start(part):
        for copy in keep(part):
            copy.start()

    def slot(t, _):
        @pl.when(t < RAW)
        def _():
            y_near(t)

        @pl.when(t + 2 < RAW)
        def _():
            @pl.when(t + 2 >= 4)
            def _():
                await_(raw.at[y, t + 2], a_recv.at[t + 3])

            send_y(t + 2)

        pl.when(t == 0)(gains_near)
        pl.when(t == 1)(gains_far)

        @pl.when((t % 2 == 1) & (t < 8))
        def _():
            z_near(t // 2)

        pl.when(t == 0)(lambda: along_x(1))
        pl.when(t == 1)(lambda: send_x(2))
        pl.when(t == 2)(lambda: send_x(3))
        pl.when(t == 2)(lambda: send_z(3, 0))
        pl.when(t == 2)(lambda: along_x(2))
        pl.when(t == 4)(lambda: along_x(3))

        @pl.when((t >= 1) & (t - 1 < RAW))
        def _():
            y_far(t - 1)
            norm(t - 1)
            send_sibling(t - 1)
            pl.when((t == 3) | (t == 4))(lambda: send_normed(t - 1))

        pl.when((t == 6) | (t == 7))(lambda: take_normed(t))

        @pl.when((t % 2 == 0) & (t >= 2))
        def _():
            z_far(t // 2 - 1)

        @pl.when((t >= 1) & (t < 8))
        def _():
            await_sibling(t - 1)

        pl.when(t == 7)(lambda: await_sibling(7))

        newest = jnp.maximum(t - 2, 0) // 2
        many = newest + 1
        fresh = jnp.where(t == 8, 8, jnp.where((t % 2 == 0) & (t >= 2), t - 1, 0))
        rest = jnp.where((t < 2) | (t == 8), 0, jnp.where(t == 7, 2 * many, many))

        def item(n, _):
            late = n - fresh
            j = jnp.where(n < fresh, newest, late % many)
            i = jnp.where(n < fresh, jnp.where(t == 8, (n + 4) % 8, n), t - 1 + late // many)
            multiply(j, i)
            pl.when((t == 8) & (n == 3))(lambda: give_start(1))
            return 0

        lax.fori_loop(0, fresh + rest, item, 0)

        @pl.when(t == 7)
        def _():
            give_start(0)
            keep_start(0)

        return 0

    lax.fori_loop(0, 9, slot, 0)
    keep_start(1)

    def drain_weights(j, _):
        block = weights.at[0, 0, 0]
        for n in range(11):
            await_(block, w_send.at[j, n])
        for n in range(11, 19):
            await_(block.at[lo], w_send.at[j, n])
        return 0

    lax.fori_loop(0, CHUNKS, drain_weights, 0)

    def drain_raw(i, _):
        block = raw.at[0, 0]
        for n in range(4):
            await_(block if n < 2 else block.at[0], y_send.at[i, n])
        return 0

    lax.fori_loop(0, RAW, drain_raw, 0)

    def drain_normed(i, _):
        await_(acts.at[0, :, 0], n_send.at[i])
        return 0

    lax.fori_loop(0, STEPS, drain_normed, 0)
    for n, ref in enumerate(
        (spare, gain_mine, gain_row, gain_row, gain_row, raw.at[0, 0], raw.at[0, 0], acts.at[0, :, 0], acts.at[0, :, 0])
    ):
        await_(ref, a_send.at[n])
    for part in range(2):
        def leave(n, src, dst, device):
            await_(src, c_send.at[n])
            await_(src, c_recv.at[n])

        give(part, leave)
        for copy in keep(part):
            copy.wait()
    for copy in stores:
        copy.wait()


def local(resid, attn, attn_tangent, probe, norm_gain, gate_weight, up_weight):
    hbm, vmem = pl.BlockSpec(memory_space=pl.ANY), pl.BlockSpec(memory_space=pltpu.VMEM)
    bf16, f32 = jnp.bfloat16, jnp.float32
    dma = pltpu.SemaphoreType.DMA
    state, state_tan, hidden, hidden_tan = pl.pallas_call(
        body,
        name="block",
        out_shape=(
            jax.ShapeDtypeStruct((TOK // SUB, SUB, FEAT), bf16),
            jax.ShapeDtypeStruct((TOK // SUB, SUB, FEAT), bf16),
            jax.ShapeDtypeStruct((TOK, HID), bf16),
            jax.ShapeDtypeStruct((TOK, HID), bf16),
        ),
        in_specs=[hbm, hbm, hbm, hbm, vmem, hbm, hbm],
        out_specs=(hbm, hbm, hbm, hbm),
        scratch_shapes=[
            pltpu.VMEM((CHUNKS, 4, 4, DEPTH, 2 * UNIT), bf16),
            pltpu.VMEM((CHUNKS, DEPTH, 2 * UNIT), bf16),
            pltpu.VMEM((STEPS, 2, 2, SUB, D), bf16),
            pltpu.VMEM((4, RAW, 2, 2, SUB, FEAT), bf16),
            pltpu.VMEM((4, 2, SUB, FEAT), bf16),
            pltpu.VMEM((4, 2, 8, FEAT), f32),
            pltpu.VMEM((2, 2, 2, HALF, HID // 2), bf16),
            pltpu.VMEM((TOK, FEAT), bf16),
            pltpu.VMEM((TOK, FEAT), bf16),
            pltpu.VMEM((TOK, FEAT), bf16),
            pltpu.VMEM((TOK, FEAT), jnp.int32),
            dma((CHUNKS, 19)), dma((CHUNKS, 19)),
            dma((RAW, 4)), dma((RAW, 4)),
            dma((STEPS,)), dma((STEPS,)),
            dma((8,)), dma((8,)),
            dma((9,)), dma((9,)),
            dma((32,)),
        ],
        compiler_params=pltpu.CompilerParams(
            collective_id=0, has_side_effects=True, vmem_limit_bytes=62 << 20
        ),
    )(resid, attn, attn_tangent, probe, norm_gain.reshape(1, FEAT), gate_weight, up_weight)
    return state.reshape(TOK, FEAT), state_tan.reshape(TOK, FEAT), hidden, hidden_tan


def solution(mesh):
    in_specs = (
        P("row", "col"),
        P("row", "col"),
        P("row", "col"),
        P("row", "col"),
        P("col"),
        P("row", "col"),
        P("row", "col"),
    )
    out_specs = (P("row", "col"), P("row", "col"), P("row", "col"), P("row", "col"))
    return jax.shard_map(local, mesh=mesh, in_specs=in_specs, out_specs=out_specs, check_vma=False)
```

time: 306 us -> 145 us (0.47)
  waiting for transfers between devices: 235 us -> 0 us
  Pallas kernels: 0 us -> 137 us
  matrix products: 36.3 us -> 0 us
  blocking collectives: 13.5 us -> 0 us
  between operations: 13.8 us -> 0.66 us
  other arithmetic: 7.1 us -> 0 us
  local copies, waits for them, and re-layouts: 0.02 us -> 6.29 us
    all_gather x3 -> x0, waiting for transfers between devices: 234 us -> none  [the longest x1 92.3 us: local(): lax.all_gather(up_weight, 'row', axis=0, tiled=True)]
    pallas_call x0 -> x1, Pallas kernels: none -> 137 us  [local(): pl.pallas_call(body, name='block', out_shape=(jax.ShapeDtypeStruct((TOK /...]
    dot_general x2 -> x0, matrix products: 36.3 us -> none  [the longest x1 19 us: local(): jnp.dot(flat, lax.all_gather(up_weight, 'row', axis=0, tiled=True), prefe...]
    psum x1 -> x0, blocking collectives: 13.5 us -> none  [local(): lax.psum((jnp.sum(yval * yval, axis=1), jnp.sum(yval * tval, axis=1)), 'c...]
    unnamed x8 -> x10, local copies, waits for them, and re-layouts: 0.02 us -> 5.03 us
  transfers between devices with their start and end apart: 3 -> 0, of which waited for: 3 -> 0; matrix products, arithmetic and copies ran while one was open for 6% -> 0% of each run, Pallas kernels for 0% -> 0%
where the time goes in v2:
time: 145 us; the launch traced here: 144 us
  Pallas kernels  137 us (94%)
  local copies, waits for them, and re-layouts  6.29 us (4%)
    pallas_call x1, Pallas kernels, local(): pl.pallas_call(body, name='block', out_shape=(jax.ShapeDtypeStruct((TOK /...  137 us
    unnamed x10, local copies, waits for them, and re-layouts  5.03 us

profile of v2, /device:TPU:1, one launch (start us, length us, event | category | flops | bytes accessed | tf_op | source)
XLA Modules:
  0.0 144.4 jit_solution(13658724082980769561)
XLA Ops:
  0.6 1.3 reshape.17.gain
  1.9 137.4 %block.1 = (bf16[8,64,768]{2,1,0:T(8,128)(2,1)}, bf16[8,64,768]{2,1,0:T(8,128)(2,1)}, bf16[512,1024]{1,0:T(8,128)(2,1)}, bf16[512,1024]{1,0:T(8,128)(2,1)}) custom-call(bf16[512,768]{1,0:T(8,128)(2,1)} %resid.1, bf16[512,768]{1,0:T(8,128)(2,1)} %attn.1, bf16[512,768]{1,0:T(8,128)(2,1)} %attn_tan.1, s32[512,768]{1,0:T(8,128)} %probe.1, ...), custom_call_target="tpu_custom_call" | custom-call | tf_op jit(solution)/shard_map/block/pallas_call | solution.py:399
  139.4 0.0 copy-start.2
  139.4 0.0 copy-start.1
  139.4 2.2 %copy.15 = bf16[512,768]{1,0:T(8,128)(2,1)} copy(bf16[512,768]{1,0:T(8,128)(2,1)} %bitcast.3) | data formatting | bytes 1572864
  141.6 0.0 copy-done.2
  141.6 0.0 copy-start
  141.6 0.9 copy.16
  142.5 0.0 copy-done.1
  142.5 1.0 copy.17
  143.4 0.0 copy-done
  143.4 1.0 copy.18
Async XLA Ops:
  139.4 2.2 %copy-start.2 = (bf16[8,64,768]{2,1,0:T(8,128)(2,1)S(1)}, bf16[8,64,768]{2,1,0:T(8,128)(2,1)}, u32[]{:S(2)}) copy-start(bf16[8,64,768]{2,1,0:T(8,128)(2,1)} %get-tuple-element.9) | copy-start | bytes 2359300
  139.4 3.1 %copy-start.1 = (bf16[512,1024]{1,0:T(8,128)(2,1)S(1)}, bf16[512,1024]{1,0:T(8,128)(2,1)}, u32[]{:S(2)}) copy-start(bf16[512,1024]{1,0:T(8,128)(2,1)} %get-tuple-element.18) | copy-start | bytes 3145732
  141.6 1.9 %copy-start = (bf16[512,1024]{1,0:T(8,128)(2,1)S(1)}, bf16[512,1024]{1,0:T(8,128)(2,1)}, u32[]{:S(2)}) copy-start(bf16[512,1024]{1,0:T(8,128)(2,1)} %get-tuple-element.19) | copy-start | bytes 3145732

commit v3 on v2

--- a/solution.py
+++ b/solution.py
@@ -16,7 +16,6 @@
 HID = 1024
 UNIT = 128
 CHUNKS = HID // 2 // UNIT
-EARLY = (CHUNKS - 1) * UNIT
 STEPS = 8
 RAW = 6
 
@@ -24,7 +23,7 @@
 def body(
     resid, attn, attn_tan, probe, gain, gate_w, up_w,
     state_out, state_tan_out, hid_out, hid_tan_out,
-    weights, others, acts, raw, spare, gains, results, in_res, in_att, in_tan, in_pro,
+    weights, others, acts, totals, raw, spare, gains, results, in_res, in_att, in_tan, in_pro,
     w_send, w_recv, y_send, y_recv, n_send, n_recv, c_send, c_recv, a_send, a_recv, loc,
 ):
     row, col = lax.axis_index("row"), lax.axis_index("col")
@@ -83,6 +82,10 @@
 
     lo, hi = pl.ds(0, DEPTH // 2), pl.ds(DEPTH // 2, DEPTH // 2)
     firsts = (0, -1, 1, 2)
+    last = CHUNKS - 1
+
+    def line(j, step):
+        return weights.at[j, (z + step + 4) % 4]
 
     def spot(j, q, step):
         return weights.at[j, (z + step + 4) % 4, (x + firsts[q] + 4) % 4]
@@ -93,29 +96,33 @@
         send(others.at[j], mine, w_send.at[j, 1], w_recv.at[j, 1], at_x(-1))
         send(mine, mine, w_send.at[j, 2], w_recv.at[j, 2], at_x(2))
 
-    def send_z(j, q):
-        block = spot(j, q, 0)
+    def send_z(j, q, block):
         send(block, block, w_send.at[j, 3 + q], w_recv.at[j, 3 + q], at_z(1))
         send(block, block, w_send.at[j, 7 + q], w_recv.at[j, 7 + q], at_z(-1))
 
     def along_x(j):
         for q in (1, 2, 3):
-            await_(spot(j, q, 0), w_recv.at[j, q - 1])
-            send_z(j, q)
+            block = spot(j, q, 0)
+            await_(block, w_recv.at[j, q - 1])
+            pl.when(j < last)(lambda: send_z(j, q, block))
+        pl.when(j == last)(lambda: send_z(j, 0, line(j, 0)))
 
     def z_near(j):
-        for q in range(4):
-            prev, nxt = spot(j, q, -1), spot(j, q, 1)
-            await_(prev, w_recv.at[j, 3 + q])
-            send(prev.at[lo], prev.at[lo], w_send.at[j, 11 + q], w_recv.at[j, 11 + q], at_z(1))
-            await_(nxt, w_recv.at[j, 7 + q])
-            send(nxt.at[hi], nxt.at[hi], w_send.at[j, 15 + q], w_recv.at[j, 15 + q], at_z(-1))
+        for step, sem, half, way in ((-1, 3, lo, 1), (1, 7, hi, -1)):
+            @pl.when(j < last)
+            def _():
+                for q in range(4):
+                    await_(spot(j, q, step), w_recv.at[j, sem + q])
+
+            pl.when(j == last)(lambda: await_(line(j, step), w_recv.at[j, sem]))
+            part = line(j, step).at[:, half]
+            n = 11 if way == 1 else 12
+            send(part, part, w_send.at[j, n], w_recv.at[j, n], at_z(way))
 
     def z_far(j):
-        for q in range(4):
-            opp = spot(j, q, 2)
-            await_(opp.at[lo], w_recv.at[j, 11 + q])
-            await_(opp.at[hi], w_recv.at[j, 15 + q])
+        opp = line(j, 2)
+        await_(opp.at[:, lo], w_recv.at[j, 11])
+        await_(opp.at[:, hi], w_recv.at[j, 12])
 
     for j in range(CHUNKS):
         for pair in staged[j]:
@@ -124,7 +131,7 @@
         if j < 2:
             send_x(j)
         if j < 3:
-            send_z(j, 0)
+            send_z(j, 0, spot(j, 0, 0))
 
     for copy in loads:
         copy.wait()
@@ -171,9 +178,10 @@
     send(gain_row, gain_row, a_send.at[2], a_recv.at[2], at_y(1))
     send(gain_row, gain_row, a_send.at[3], a_recv.at[3], at_y(-1))
     send_y(1)
-    along_x(0)
-    for s in range(2):
-        send(raw.at[y, s], raw.at[y, 4 + s], a_send.at[5 + s], a_recv.at[5 + s], x_to)
+
+    def send_raw():
+        for s in (2, 3):
+            send(raw.at[y, s], raw.at[y, 2 + s], a_send.at[3 + s], a_recv.at[3 + s], x_to)
 
     prev_y, next_y, opp_y = (y + 3) % 4, (y + 1) % 4, (y + 2) % 4
 
@@ -230,32 +238,50 @@
         await_(acts.at[i, :, 1 - core], n_recv.at[i])
 
     def send_normed(i):
-        send(acts.at[i, :, core], acts.at[i + 4, :, core], a_send.at[5 + i], a_recv.at[5 + i], x_to)
+        send(acts.at[i, :, core], acts.at[i + 6, :, core], a_send.at[7 + i], a_recv.at[7 + i], x_to)
 
     def take_normed(i):
         await_(acts.at[i, :, core], a_recv.at[1 + i])
         send_sibling(i)
 
-    def multiply(j, i):
-        out = jnp.dot(
-            acts[i].reshape(4 * SUB, D), weights[j].reshape(D, 2 * UNIT), preferred_element_type=jnp.float32
-        )
-        gate, upper = out[: 2 * SUB, :UNIT], out[: 2 * SUB, UNIT:]
-        gate_t, upper_t = out[2 * SUB :, :UNIT], out[2 * SUB :, UNIT:]
-        sig = jax.nn.sigmoid(gate)
-        active = gate * sig
-        slope = sig * (1.0 + gate * (1.0 - sig))
+    ROWS = 4 * SUB
+
+    def finish(j, p, out):
         cols = pl.ds(pl.multiple_of(j * UNIT, UNIT), UNIT)
-        rows = pl.ds(pl.multiple_of((i % 4) * SUB, SUB), SUB)
-        whose = i // 4
-        hidden = (active * upper).astype(jnp.bfloat16)
-        hidden_tan = (slope * gate_t * upper + active * upper_t).astype(jnp.bfloat16)
-        for c in range(2):
-            results[whose, 0, c, rows, cols] = hidden[c * SUB : (c + 1) * SUB]
-            results[whose, 1, c, rows, cols] = hidden_tan[c * SUB : (c + 1) * SUB]
+        for s in range(2):
+            vals, tans = out[s * ROWS : s * ROWS + ROWS // 2], out[s * ROWS + ROWS // 2 : (s + 1) * ROWS]
+            gate, upper = vals[:, :UNIT], vals[:, UNIT:]
+            gate_t, upper_t = tans[:, :UNIT], tans[:, UNIT:]
+            sig = jax.nn.sigmoid(gate)
+            active = gate * sig
+            slope = sig * (1.0 + gate * (1.0 - sig))
+            hidden = (active * upper).astype(jnp.bfloat16)
+            hidden_tan = (slope * gate_t * upper + active * upper_t).astype(jnp.bfloat16)
+            rows = pl.ds(pl.multiple_of((p + p // 2) % 2 * 2 * SUB + s * SUB, SUB), SUB)
+            for c in range(2):
+                results[p // 2, 0, c, rows, cols] = hidden[c * SUB : (c + 1) * SUB]
+                results[p // 2, 1, c, rows, cols] = hidden_tan[c * SUB : (c + 1) * SUB]
+
+    def multiply(j, p):
+        lhs, rhs = acts[pl.ds(2 * p, 2)].reshape(2 * ROWS, D), weights[j].reshape(D, 2 * UNIT)
+        finish(j, p, jnp.dot(lhs, rhs, preferred_element_type=jnp.float32))
+
+    def part(j, p, step):
+        where = (z + step + 4) % 4
+        cols = pl.ds(pl.multiple_of(where * (D // 4), D // 4), D // 4)
+        lhs = acts[pl.ds(2 * p, 2), :, :, :, cols].reshape(2 * ROWS, D // 4)
+        return jnp.dot(lhs, weights[j, where].reshape(D // 4, 2 * UNIT), preferred_element_type=jnp.float32)
+
+    def multiply_near(j, p):
+        totals[j % 2, p] = part(j, p, 0) + part(j, p, -1) + part(j, p, 1)
+
+    def multiply_far(j, p):
+        finish(j, p, totals[j % 2, p] + part(j, p, 2))
+
+    parts = ((0, 2 * UNIT), (2 * UNIT, UNIT), (3 * UNIT, UNIT))
 
     def give(part, do):
-        begin, width = (0, EARLY) if part == 0 else (EARLY, UNIT)
+        begin, width = parts[part]
         here = pl.ds(begin, width)
         there = pl.ds(pl.multiple_of(parity * (HID // 2) + begin, UNIT), width)
         for k, out in enumerate((hid_out, hid_tan_out)):
@@ -267,7 +293,7 @@
         give(part, lambda n, src, dst, device: send(src, dst, c_send.at[n], c_recv.at[n], device))
 
     def keep(part):
-        begin, width = (0, EARLY) if part == 0 else (EARLY, UNIT)
+        begin, width = parts[part]
         there = pl.ds(pl.multiple_of(parity * (HID // 2) + begin, UNIT), width)
         return [
             pltpu.make_async_copy(
@@ -282,83 +308,131 @@
         for copy in keep(part):
             copy.start()
 
-    def slot(t, _):
-        @pl.when(t < RAW)
-        def _():
-            y_near(t)
-
-        @pl.when(t + 2 < RAW)
-        def _():
-            @pl.when(t + 2 >= 4)
+    kinds = ("y_far", "y_near", "along_x", "z_near", "z_far", "take", "sibling")
+    whole, near, far = 0, 1, 2
+    plan = (
+        (dict(along_x=0), ()),
+        (dict(y_near=0), ()),
+        (dict(along_x=1), ()),
+        (dict(y_far=0, y_near=1, z_near=0), ()),
+        (dict(along_x=2), ()),
+        (dict(y_far=1, y_near=2, z_near=1), ()),
+        (dict(along_x=3), ()),
+        (dict(z_far=0, sibling=0), ((whole, 0, (0,)),)),
+        (dict(y_far=2, y_near=3), ()),
+        (dict(z_near=2), ((near, 2, (0,)),)),
+        (dict(take=6), ()),
+        (dict(y_far=3, y_near=4), ()),
+        (dict(z_far=1), ((whole, 1, (0,)),)),
+        (dict(sibling=1), ((whole, 0, (1,)), (whole, 1, (1,)))),
+        (dict(take=7), ((near, 2, (1,)),)),
+        (dict(y_far=4, y_near=5), ()),
+        (dict(sibling=3), ((whole, 0, (3,)), (whole, 1, (3,)), (near, 2, (3,)))),
+        (dict(y_far=5), ()),
+        (dict(z_near=3), ((near, 3, (0, 1, 3)),)),
+        (dict(sibling=2), ((whole, 0, (2,)), (whole, 1, (2,)))),
+        (dict(), ((near, 2, (2,)), (near, 3, (2,)))),
+        (dict(z_far=2), ((far, 2, (2, 3, 0, 1)),)),
+        (dict(z_far=3), ((far, 3, (2, 3, 0, 1)),)),
+    )
+    slots = [sum((e.get(k, -1) + 1) << 4 * n for n, k in enumerate(kinds)) for e, _ in plan]
+    items = [[how << 4 | j << 2 | p for how, j, pairs in todo for p in pairs] for _, todo in plan]
+    codes = [code for todo in items for code in todo]
+    bounds = [sum(len(todo) for todo in items[:u]) for u in range(len(items) + 1)]
+
+    def pick(values, n):
+        out = jnp.int32(values[0])
+        for at in range(1, len(values)):
+            if values[at] != values[at - 1]:
+                out = jnp.where(n >= at, jnp.int32(values[at]), out)
+        return out
+
+    def slot(u, begin):
+        code = pick(slots, u)
+
+        def event(kind):
+            def run(act):
+                index = (lax.shift_right_logical(code, jnp.int32(4 * kinds.index(kind))) & 15) - 1
+                pl.when(index >= 0)(lambda: act(index))
+
+            return run
+
+        @event("y_far")
+        def _(i):
+            y_far(i)
+            pl.when(i == 0)(gains_far)
+            norm(i)
+            send_sibling(i)
+            pl.when(i < 2)(lambda: send_normed(i))
+
+        @event("y_near")
+        def _(i):
+            y_near(i)
+            pl.when(i == 0)(gains_near)
+
+            @pl.when(i + 2 < RAW)
             def _():
-                await_(raw.at[y, t + 2], a_recv.at[t + 3])
-
-            send_y(t + 2)
-
-        pl.when(t == 0)(gains_near)
-        pl.when(t == 1)(gains_far)
-
-        @pl.when((t % 2 == 1) & (t < 8))
-        def _():
-            z_near(t // 2)
-
-        pl.when(t == 0)(lambda: along_x(1))
-        pl.when(t == 1)(lambda: send_x(2))
-        pl.when(t == 2)(lambda: send_x(3))
-        pl.when(t == 2)(lambda: send_z(3, 0))
-        pl.when(t == 2)(lambda: along_x(2))
-        pl.when(t == 4)(lambda: along_x(3))
-
-        @pl.when((t >= 1) & (t - 1 < RAW))
-        def _():
-            y_far(t - 1)
-            norm(t - 1)
-            send_sibling(t - 1)
-            pl.when((t == 3) | (t == 4))(lambda: send_normed(t - 1))
-
-        pl.when((t == 6) | (t == 7))(lambda: take_normed(t))
-
-        @pl.when((t % 2 == 0) & (t >= 2))
-        def _():
-            z_far(t // 2 - 1)
-
-        @pl.when((t >= 1) & (t < 8))
-        def _():
-            await_sibling(t - 1)
-
-        pl.when(t == 7)(lambda: await_sibling(7))
-
-        newest = jnp.maximum(t - 2, 0) // 2
-        many = newest + 1
-        fresh = jnp.where(t == 8, 8, jnp.where((t % 2 == 0) & (t >= 2), t - 1, 0))
-        rest = jnp.where((t < 2) | (t == 8), 0, jnp.where(t == 7, 2 * many, many))
+                pl.when(i >= 2)(lambda: await_(raw.at[y, i + 2], a_recv.at[i + 3]))
+                send_y(i + 2)
+
+        @event("along_x")
+        def _(j):
+            along_x(j)
+
+            @pl.when(j == 0)
+            def _():
+                send_x(2)
+                send_raw()
+
+            pl.when(j == 1)(lambda: send_x(3))
+
+        event("z_near")(z_near)
+        event("z_far")(z_far)
+        event("take")(take_normed)
+
+        @event("sibling")
+        def _(p):
+            await_sibling(2 * p)
+            await_sibling(2 * p + 1)
 
         def item(n, _):
-            late = n - fresh
-            j = jnp.where(n < fresh, newest, late % many)
-            i = jnp.where(n < fresh, jnp.where(t == 8, (n + 4) % 8, n), t - 1 + late // many)
-            multiply(j, i)
-            pl.when((t == 8) & (n == 3))(lambda: give_start(1))
+            what = pick(codes, n)
+            how, j, p = lax.shift_right_logical(what, jnp.int32(4)), lax.shift_right_logical(what, jnp.int32(2)) & 3, what & 3
+            pl.when(how == whole)(lambda: multiply(j, p))
+            pl.when(how == near)(lambda: multiply_near(j, p))
+            pl.when(how == far)(lambda: multiply_far(j, p))
+            pl.when(n == bounds[-3] + 1)(lambda: give_start(1))
+            pl.when(n == bounds[-2] + 1)(lambda: give_start(2))
             return 0
 
-        lax.fori_loop(0, fresh + rest, item, 0)
-
-        @pl.when(t == 7)
+        end = pick(bounds[1:], u)
+        lax.fori_loop(begin, end, item, 0)
+
+        @pl.when(u == len(plan) - 4)
         def _():
             give_start(0)
             keep_start(0)
 
-        return 0
-
-    lax.fori_loop(0, 9, slot, 0)
-    keep_start(1)
+        pl.when(u == len(plan) - 2)(lambda: keep_start(1))
+        return end
+
+    lax.fori_loop(0, len(plan), slot, jnp.int32(0))
+    keep_start(2)
 
     def drain_weights(j, _):
-        block = weights.at[0, 0, 0]
-        for n in range(11):
+        block, whole_line = weights.at[0, 0, 0], weights.at[0, 0]
+        for n in range(3):
             await_(block, w_send.at[j, n])
-        for n in range(11, 19):
-            await_(block.at[lo], w_send.at[j, n])
+        for n in (3, 7):
+            pl.when(j == last)(lambda: await_(whole_line, w_send.at[j, n]))
+
+            @pl.when(j < last)
+            def _():
+                for q in range(4):
+                    await_(block, w_send.at[j, n + q])
+
+        for n in (11, 12):
+            await_(whole_line.at[:, lo], w_send.at[j, n])
         return 0
 
     lax.fori_loop(0, CHUNKS, drain_weights, 0)
@@ -380,7 +454,7 @@
         (spare, gain_mine, gain_row, gain_row, gain_row, raw.at[0, 0], raw.at[0, 0], acts.at[0, :, 0], acts.at[0, :, 0])
     ):
         await_(ref, a_send.at[n])
-    for part in range(2):
+    for part in range(3):
         def leave(n, src, dst, device):
             await_(src, c_send.at[n])
             await_(src, c_recv.at[n])
@@ -411,6 +485,7 @@
             pltpu.VMEM((CHUNKS, 4, 4, DEPTH, 2 * UNIT), bf16),
             pltpu.VMEM((CHUNKS, DEPTH, 2 * UNIT), bf16),
             pltpu.VMEM((STEPS, 2, 2, SUB, D), bf16),
+            pltpu.VMEM((2, STEPS // 2, 8 * SUB, 2 * UNIT), f32),
             pltpu.VMEM((4, RAW, 2, 2, SUB, FEAT), bf16),
             pltpu.VMEM((4, 2, SUB, FEAT), bf16),
             pltpu.VMEM((4, 2, 8, FEAT), f32),
@@ -419,12 +494,12 @@
             pltpu.VMEM((TOK, FEAT), bf16),
             pltpu.VMEM((TOK, FEAT), bf16),
             pltpu.VMEM((TOK, FEAT), jnp.int32),
-            dma((CHUNKS, 19)), dma((CHUNKS, 19)),
+            dma((CHUNKS, 13)), dma((CHUNKS, 13)),
             dma((RAW, 4)), dma((RAW, 4)),
             dma((STEPS,)), dma((STEPS,)),
-            dma((8,)), dma((8,)),
+            dma((12,)), dma((12,)),
             dma((9,)), dma((9,)),
-            dma((32,)),
+            dma((36,)),
         ],
         compiler_params=pltpu.CompilerParams(
             collective_id=0, has_side_effects=True, vmem_limit_bytes=62 << 20

time: 145 us -> 127 us (0.88)
  Pallas kernels: 137 us -> 120 us
    pallas_call x1, Pallas kernels: 137 us -> 120 us  [local(): pl.pallas_call(body, name='block', out_shape=(jax.ShapeDtypeStruct((TOK /...]
where the time goes in v3:
time: 127 us
  Pallas kernels  120 us (94%)
  local copies, waits for them, and re-layouts  6.29 us (5%)
    pallas_call x1, Pallas kernels, local(): pl.pallas_call(body, name='block', out_shape=(jax.ShapeDtypeStruct((TOK /...  120 us
    unnamed x10, local copies, waits for them, and re-layouts  5.03 us

profile of v3, /device:TPU:1, one launch (start us, length us, event | category | flops | bytes accessed | tf_op | source)
XLA Modules:
  0.0 127.2 jit_solution(11095996484178608053)
XLA Ops:
  0.6 1.3 reshape.17.gain
  1.9 120.3 %block.1 = (bf16[8,64,768]{2,1,0:T(8,128)(2,1)}, bf16[8,64,768]{2,1,0:T(8,128)(2,1)}, bf16[512,1024]{1,0:T(8,128)(2,1)}, bf16[512,1024]{1,0:T(8,128)(2,1)}) custom-call(bf16[512,768]{1,0:T(8,128)(2,1)} %resid.1, bf16[512,768]{1,0:T(8,128)(2,1)} %attn.1, bf16[512,768]{1,0:T(8,128)(2,1)} %attn_tan.1, s32[512,768]{1,0:T(8,128)} %probe.1, ...), custom_call_target="tpu_custom_call" | custom-call | tf_op jit(solution)/shard_map/block/pallas_call | solution.py:473
  122.2 0.0 copy-start.2
  122.2 0.0 copy-start.1
  122.2 2.2 %copy.15 = bf16[512,768]{1,0:T(8,128)(2,1)} copy(bf16[512,768]{1,0:T(8,128)(2,1)} %bitcast.3) | data formatting | bytes 1572864
  124.4 0.0 copy-done.2
  124.4 0.0 copy-start
  124.4 0.9 copy.16
  125.3 0.0 copy-done.1
  125.3 1.0 copy.17
  126.3 0.0 copy-done
  126.3 1.0 copy.18
Async XLA Ops:
  122.2 2.2 %copy-start.2 = (bf16[8,64,768]{2,1,0:T(8,128)(2,1)S(1)}, bf16[8,64,768]{2,1,0:T(8,128)(2,1)}, u32[]{:S(2)}) copy-start(bf16[8,64,768]{2,1,0:T(8,128)(2,1)} %get-tuple-element.9) | copy-start | bytes 2359300
  122.2 3.1 %copy-start.1 = (bf16[512,1024]{1,0:T(8,128)(2,1)S(1)}, bf16[512,1024]{1,0:T(8,128)(2,1)}, u32[]{:S(2)}) copy-start(bf16[512,1024]{1,0:T(8,128)(2,1)} %get-tuple-element.18) | copy-start | bytes 3145732
  124.4 1.9 %copy-start = (bf16[512,1024]{1,0:T(8,128)(2,1)S(1)}, bf16[512,1024]{1,0:T(8,128)(2,1)}, u32[]{:S(2)}) copy-start(bf16[512,1024]{1,0:T(8,128)(2,1)} %get-tuple-element.19) | copy-start | bytes 3145732

commit v4 on v3

--- a/solution.py
+++ b/solution.py
@@ -135,7 +135,7 @@
 
     for copy in loads:
         copy.wait()
-    gains[y, core] = jnp.broadcast_to(gain[...], (8, FEAT))
+    gains[y, core] = jnp.broadcast_to(gain[...].reshape(1, FEAT), (8, FEAT))
 
     def add(half, target):
         def step(s, _):
@@ -320,9 +320,8 @@
         (dict(along_x=3), ()),
         (dict(z_far=0, sibling=0), ((whole, 0, (0,)),)),
         (dict(y_far=2, y_near=3), ()),
-        (dict(z_near=2), ((near, 2, (0,)),)),
         (dict(take=6), ()),
-        (dict(y_far=3, y_near=4), ()),
+        (dict(z_near=2, y_far=3, y_near=4), ((near, 2, (0,)),)),
         (dict(z_far=1), ((whole, 1, (0,)),)),
         (dict(sibling=1), ((whole, 0, (1,)), (whole, 1, (1,)))),
         (dict(take=7), ((near, 2, (1,)),)),
@@ -332,8 +331,8 @@
         (dict(z_near=3), ((near, 3, (0, 1, 3)),)),
         (dict(sibling=2), ((whole, 0, (2,)), (whole, 1, (2,)))),
         (dict(), ((near, 2, (2,)), (near, 3, (2,)))),
-        (dict(z_far=2), ((far, 2, (2, 3, 0, 1)),)),
-        (dict(z_far=3), ((far, 3, (2, 3, 0, 1)),)),
+        (dict(z_far=2), ((far, 2, (2, 3)),)),
+        (dict(z_far=3), ((far, 3, (2, 3)), (far, 2, (0, 1)), (far, 3, (0, 1)))),
     )
     slots = [sum((e.get(k, -1) + 1) << 4 * n for n, k in enumerate(kinds)) for e, _ in plan]
     items = [[how << 4 | j << 2 | p for how, j, pairs in todo for p in pairs] for _, todo in plan]
@@ -413,10 +412,10 @@
             give_start(0)
             keep_start(0)
 
-        pl.when(u == len(plan) - 2)(lambda: keep_start(1))
         return end
 
     lax.fori_loop(0, len(plan), slot, jnp.int32(0))
+    keep_start(1)
     keep_start(2)
 
     def drain_weights(j, _):
@@ -466,11 +465,32 @@
         copy.wait()
 
 
+def settle(*refs):
+    ins, outs, held, sems = refs[:4], refs[4:8], refs[8:12], refs[12]
+    pieces = []
+    for n in range(4):
+        for half in range(2):
+            size = ins[n].shape[0] // 2
+            rows = pl.ds(half * size, size)
+            k = 2 * n + half
+            pieces.append((
+                pltpu.make_async_copy(ins[n].at[rows], held[n].at[rows], sems.at[0, k]),
+                pltpu.make_async_copy(held[n].at[rows], outs[n].at[rows], sems.at[1, k]),
+            ))
+    for get, _ in pieces:
+        get.start()
+    for get, put in pieces:
+        get.wait()
+        put.start()
+    for _, put in pieces:
+        put.wait()
+
+
 def local(resid, attn, attn_tangent, probe, norm_gain, gate_weight, up_weight):
     hbm, vmem = pl.BlockSpec(memory_space=pl.ANY), pl.BlockSpec(memory_space=pltpu.VMEM)
     bf16, f32 = jnp.bfloat16, jnp.float32
     dma = pltpu.SemaphoreType.DMA
-    state, state_tan, hidden, hidden_tan = pl.pallas_call(
+    found = pl.pallas_call(
         body,
         name="block",
         out_shape=(
@@ -504,7 +524,16 @@
         compiler_params=pltpu.CompilerParams(
             collective_id=0, has_side_effects=True, vmem_limit_bytes=62 << 20
         ),
-    )(resid, attn, attn_tangent, probe, norm_gain.reshape(1, FEAT), gate_weight, up_weight)
+    )(resid, attn, attn_tangent, probe, norm_gain, gate_weight, up_weight)
+    state, state_tan, hidden, hidden_tan = pl.pallas_call(
+        settle,
+        name="settle",
+        out_shape=tuple(jax.ShapeDtypeStruct(a.shape, a.dtype) for a in found),
+        in_specs=[hbm] * 4,
+        out_specs=(hbm,) * 4,
+        scratch_shapes=[*(pltpu.VMEM(a.shape, a.dtype) for a in found), dma((2, 8))],
+        compiler_params=pltpu.CompilerParams(vmem_limit_bytes=62 << 20),
+    )(*found)
     return state.reshape(TOK, FEAT), state_tan.reshape(TOK, FEAT), hidden, hidden_tan
 
 

time: 127 us -> 124 us (0.976)
  local copies, waits for them, and re-layouts: 6.29 us -> 0 us
  Pallas kernels: 120 us -> 123 us
    unnamed x10 -> x0, local copies, waits for them, and re-layouts: 5.03 us -> none
    pallas_call x0 -> x1, Pallas kernels: none -> 3.14 us  [local(): pl.pallas_call(settle, name='settle', out_shape=tuple((jax.ShapeDtypeStru...]
where the time goes in v4:
time: 124 us
  Pallas kernels  123 us (99%)
    pallas_call x1, Pallas kernels, local(): pl.pallas_call(body, name='block', out_shape=(jax.ShapeDtypeStruct((TOK /...  120 us
    pallas_call x1, Pallas kernels, local(): pl.pallas_call(settle, name='settle', out_shape=tuple((jax.ShapeDtypeStru...  3.14 us

profile of v4, /device:TPU:1, one launch (start us, length us, event | category | flops | bytes accessed | tf_op | source)
XLA Modules:
  0.0 124.1 jit_solution(16512881678571444118)
XLA Ops:
  0.6 120.3 %block.1 = (bf16[8,64,768]{2,1,0:T(8,128)(2,1)}, bf16[8,64,768]{2,1,0:T(8,128)(2,1)}, bf16[512,1024]{1,0:T(8,128)(2,1)}, bf16[512,1024]{1,0:T(8,128)(2,1)}) custom-call(bf16[512,768]{1,0:T(8,128)(2,1)} %resid.1, bf16[512,768]{1,0:T(8,128)(2,1)} %attn.1, bf16[512,768]{1,0:T(8,128)(2,1)} %attn_tan.1, s32[512,768]{1,0:T(8,128)} %probe.1, f32[768]{0:T(1024)} %gain.1, ...), custom_call_target="tpu_custom_call" | custom-call | tf_op jit(solution)/shard_map/block/pallas_call | solution.py:493
  121.0 3.1 %settle.1 = (bf16[8,64,768]{2,1,0:T(8,128)(2,1)}, bf16[8,64,768]{2,1,0:T(8,128)(2,1)}, bf16[512,1024]{1,0:T(8,128)(2,1)}, bf16[512,1024]{1,0:T(8,128)(2,1)}) custom-call(bf16[8,64,768]{2,1,0:T(8,128)(2,1)} %get-tuple-element.12.refs_0_, bf16[8,64,768]{2,1,0:T(8,128)(2,1)} %get-tuple-element.13.refs_1_, bf16[512,1024]{1,0:T(8,128)(2,1)} %get-tuple-element.14.refs_2_, ...), custom_call_target="tpu_custom_call" | custom-call | tf_op jit(solution)/shard_map/settle/pallas_call | solution.py:528

commit v5 on v4

--- a/solution.py
+++ b/solution.py
@@ -50,6 +50,10 @@
 
     def await_(ref, sem):
         pltpu.make_async_copy(ref, ref, sem).wait()
+
+    barrier = pltpu.get_barrier_semaphore()
+    for other in (at_x(1), at_x(-1), at_x(2), at_y(1), at_y(-1), at_z(1), at_z(-1), sibling):
+        pl.semaphore_signal(barrier, inc=1, device_id=other, device_id_type=MESH)
 
     def stage(j, n, half, target):
         cols = pl.ds(pl.multiple_of(half * (HID // 2) + j * UNIT, UNIT), UNIT)
@@ -75,9 +79,6 @@
     for copy in loads:
         copy.start()
 
-    barrier = pltpu.get_barrier_semaphore()
-    for other in (at_x(1), at_x(-1), at_x(2), at_y(1), at_y(-1), at_z(1), at_z(-1), sibling):
-        pl.semaphore_signal(barrier, inc=1, device_id=other, device_id_type=MESH)
     pl.semaphore_wait(barrier, 8)
 
     lo, hi = pl.ds(0, DEPTH // 2), pl.ds(DEPTH // 2, DEPTH // 2)
@@ -128,10 +129,10 @@
         for pair in staged[j]:
             for copy in pair:
                 copy.wait()
+        if j < 3:
+            send_z(j, 0, spot(j, 0, 0))
         if j < 2:
             send_x(j)
-        if j < 3:
-            send_z(j, 0, spot(j, 0, 0))
 
     for copy in loads:
         copy.wait()
@@ -246,37 +247,41 @@
 
     ROWS = 4 * SUB
 
-    def finish(j, p, out):
+    def finish(j, i, out):
+        gate, upper = out[: ROWS // 2, :UNIT], out[: ROWS // 2, UNIT:]
+        gate_t, upper_t = out[ROWS // 2 :, :UNIT], out[ROWS // 2 :, UNIT:]
+        sig = jax.nn.sigmoid(gate)
+        active = gate * sig
+        slope = sig * (1.0 + gate * (1.0 - sig))
+        hidden = (active * upper).astype(jnp.bfloat16)
+        hidden_tan = (slope * gate_t * upper + active * upper_t).astype(jnp.bfloat16)
+        whose = i // 4
         cols = pl.ds(pl.multiple_of(j * UNIT, UNIT), UNIT)
-        for s in range(2):
-            vals, tans = out[s * ROWS : s * ROWS + ROWS // 2], out[s * ROWS + ROWS // 2 : (s + 1) * ROWS]
-            gate, upper = vals[:, :UNIT], vals[:, UNIT:]
-            gate_t, upper_t = tans[:, :UNIT], tans[:, UNIT:]
-            sig = jax.nn.sigmoid(gate)
-            active = gate * sig
-            slope = sig * (1.0 + gate * (1.0 - sig))
-            hidden = (active * upper).astype(jnp.bfloat16)
-            hidden_tan = (slope * gate_t * upper + active * upper_t).astype(jnp.bfloat16)
-            rows = pl.ds(pl.multiple_of((p + p // 2) % 2 * 2 * SUB + s * SUB, SUB), SUB)
-            for c in range(2):
-                results[p // 2, 0, c, rows, cols] = hidden[c * SUB : (c + 1) * SUB]
-                results[p // 2, 1, c, rows, cols] = hidden_tan[c * SUB : (c + 1) * SUB]
-
-    def multiply(j, p):
-        lhs, rhs = acts[pl.ds(2 * p, 2)].reshape(2 * ROWS, D), weights[j].reshape(D, 2 * UNIT)
-        finish(j, p, jnp.dot(lhs, rhs, preferred_element_type=jnp.float32))
-
-    def part(j, p, step):
+        rows = pl.ds(pl.multiple_of((i + 2 * whose) % 4 * SUB, SUB), SUB)
+        for c in range(2):
+            results[whose, 0, c, rows, cols] = hidden[c * SUB : (c + 1) * SUB]
+            results[whose, 1, c, rows, cols] = hidden_tan[c * SUB : (c + 1) * SUB]
+
+    def multiply(j, i, count):
+        lhs, rhs = acts[pl.ds(i, count)].reshape(count * ROWS, D), weights[j].reshape(D, 2 * UNIT)
+        out = jnp.dot(lhs, rhs, preferred_element_type=jnp.float32)
+        for s in range(count):
+            finish(j, i + s, out[s * ROWS : (s + 1) * ROWS])
+
+    def part(j, i, count, step):
         where = (z + step + 4) % 4
         cols = pl.ds(pl.multiple_of(where * (D // 4), D // 4), D // 4)
-        lhs = acts[pl.ds(2 * p, 2), :, :, :, cols].reshape(2 * ROWS, D // 4)
+        lhs = acts[pl.ds(i, count), :, :, :, cols].reshape(count * ROWS, D // 4)
         return jnp.dot(lhs, weights[j, where].reshape(D // 4, 2 * UNIT), preferred_element_type=jnp.float32)
 
-    def multiply_near(j, p):
-        totals[j % 2, p] = part(j, p, 0) + part(j, p, -1) + part(j, p, 1)
-
-    def multiply_far(j, p):
-        finish(j, p, totals[j % 2, p] + part(j, p, 2))
+    def multiply_near(j, i, count):
+        out = part(j, i, count, 0) + part(j, i, count, -1) + part(j, i, count, 1)
+        totals[j % 2, pl.ds(i, count)] = out.reshape(count, ROWS, 2 * UNIT)
+
+    def multiply_far(j, i, count):
+        out = totals[j % 2, pl.ds(i, count)].reshape(count * ROWS, 2 * UNIT) + part(j, i, count, 2)
+        for s in range(count):
+            finish(j, i + s, out[s * ROWS : (s + 1) * ROWS])
 
     parts = ((0, 2 * UNIT), (2 * UNIT, UNIT), (3 * UNIT, UNIT))
 
@@ -309,7 +314,7 @@
             copy.start()
 
     kinds = ("y_far", "y_near", "along_x", "z_near", "z_far", "take", "sibling")
-    whole, near, far = 0, 1, 2
+    whole, near, far, whole_pair, near_pair = 0, 1, 2, 3, 4
     plan = (
         (dict(along_x=0), ()),
         (dict(y_near=0), ()),
@@ -318,24 +323,28 @@
         (dict(along_x=2), ()),
         (dict(y_far=1, y_near=2, z_near=1), ()),
         (dict(along_x=3), ()),
-        (dict(z_far=0, sibling=0), ((whole, 0, (0,)),)),
+        (dict(z_far=0, sibling=0), ()),
+        (dict(sibling=1), ((whole_pair, 0, (0,)),)),
         (dict(y_far=2, y_near=3), ()),
-        (dict(take=6), ()),
-        (dict(z_near=2, y_far=3, y_near=4), ((near, 2, (0,)),)),
-        (dict(z_far=1), ((whole, 1, (0,)),)),
-        (dict(sibling=1), ((whole, 0, (1,)), (whole, 1, (1,)))),
-        (dict(take=7), ((near, 2, (1,)),)),
+        (dict(sibling=2), ((whole, 0, (2,)),)),
+        (dict(z_near=2, take=6), ((near_pair, 2, (0,)), (near, 2, (2,)))),
+        (dict(sibling=6), ((whole, 0, (6,)), (near, 2, (6,)))),
+        (dict(y_far=3, y_near=4), ()),
+        (dict(z_far=1), ((whole_pair, 1, (0,)), (whole, 1, (2, 6)))),
+        (dict(sibling=3), ((whole, 0, (3,)), (whole, 1, (3,)), (near, 2, (3,)))),
+        (dict(take=7), ()),
         (dict(y_far=4, y_near=5), ()),
-        (dict(sibling=3), ((whole, 0, (3,)), (whole, 1, (3,)), (near, 2, (3,)))),
+        (dict(sibling=7), ((whole, 0, (7,)), (whole, 1, (7,)), (near, 2, (7,)))),
+        (dict(sibling=4), ((whole, 0, (4,)), (whole, 1, (4,)), (near, 2, (4,)))),
         (dict(y_far=5), ()),
-        (dict(z_near=3), ((near, 3, (0, 1, 3)),)),
-        (dict(sibling=2), ((whole, 0, (2,)), (whole, 1, (2,)))),
-        (dict(), ((near, 2, (2,)), (near, 3, (2,)))),
-        (dict(z_far=2), ((far, 2, (2, 3)),)),
-        (dict(z_far=3), ((far, 3, (2, 3)), (far, 2, (0, 1)), (far, 3, (0, 1)))),
+        (dict(z_near=3), ((near_pair, 3, (0, 2, 6)),)),
+        (dict(sibling=5), ((whole, 0, (5,)), (whole, 1, (5,)))),
+        (dict(), ((near, 2, (5,)), (near_pair, 3, (4,)))),
+        (dict(z_far=2), ((far, 2, (4, 6)),)),
+        (dict(z_far=3), ((far, 3, (4, 6)), (far, 2, (0, 2)), (far, 3, (0, 2)))),
     )
     slots = [sum((e.get(k, -1) + 1) << 4 * n for n, k in enumerate(kinds)) for e, _ in plan]
-    items = [[how << 4 | j << 2 | p for how, j, pairs in todo for p in pairs] for _, todo in plan]
+    items = [[how << 5 | j << 3 | i for how, j, steps in todo for i in steps] for _, todo in plan]
     codes = [code for todo in items for code in todo]
     bounds = [sum(len(todo) for todo in items[:u]) for u in range(len(items) + 1)]
 
@@ -389,17 +398,16 @@
         event("z_far")(z_far)
         event("take")(take_normed)
 
-        @event("sibling")
-        def _(p):
-            await_sibling(2 * p)
-            await_sibling(2 * p + 1)
+        event("sibling")(await_sibling)
 
         def item(n, _):
             what = pick(codes, n)
-            how, j, p = lax.shift_right_logical(what, jnp.int32(4)), lax.shift_right_logical(what, jnp.int32(2)) & 3, what & 3
-            pl.when(how == whole)(lambda: multiply(j, p))
-            pl.when(how == near)(lambda: multiply_near(j, p))
-            pl.when(how == far)(lambda: multiply_far(j, p))
+            how, j, i = lax.shift_right_logical(what, jnp.int32(5)), lax.shift_right_logical(what, jnp.int32(3)) & 3, what & 7
+            pl.when(how == whole)(lambda: multiply(j, i, 1))
+            pl.when(how == near)(lambda: multiply_near(j, i, 1))
+            pl.when(how == far)(lambda: multiply_far(j, i, 2))
+            pl.when(how == whole_pair)(lambda: multiply(j, i, 2))
+            pl.when(how == near_pair)(lambda: multiply_near(j, i, 2))
             pl.when(n == bounds[-3] + 1)(lambda: give_start(1))
             pl.when(n == bounds[-2] + 1)(lambda: give_start(2))
             return 0
@@ -505,7 +513,7 @@
             pltpu.VMEM((CHUNKS, 4, 4, DEPTH, 2 * UNIT), bf16),
             pltpu.VMEM((CHUNKS, DEPTH, 2 * UNIT), bf16),
             pltpu.VMEM((STEPS, 2, 2, SUB, D), bf16),
-            pltpu.VMEM((2, STEPS // 2, 8 * SUB, 2 * UNIT), f32),
+            pltpu.VMEM((2, STEPS, 4 * SUB, 2 * UNIT), f32),
             pltpu.VMEM((4, RAW, 2, 2, SUB, FEAT), bf16),
             pltpu.VMEM((4, 2, SUB, FEAT), bf16),
             pltpu.VMEM((4, 2, 8, FEAT), f32),

time: 124 us -> 123 us (level); the launches traced: 124 us -> 122 us
  Pallas kernels: 123 us -> 121 us
    pallas_call x1, Pallas kernels: 120 us -> 118 us  [local(): pl.pallas_call(body, name='block', out_shape=(jax.ShapeDtypeStruct((TOK /...]
where the time goes in v5:
time: 123 us; the launch traced here: 122 us
  Pallas kernels  121 us (98%)
    pallas_call x1, Pallas kernels, local(): pl.pallas_call(body, name='block', out_shape=(jax.ShapeDtypeStruct((TOK /...  118 us
    pallas_call x1, Pallas kernels, local(): pl.pallas_call(settle, name='settle', out_shape=tuple((jax.ShapeDtypeStru...  3.14 us

profile of v5, /device:TPU:1, one launch (start us, length us, event | category | flops | bytes accessed | tf_op | source)
XLA Modules:
  0.0 121.7 jit_solution(15630671447043188290)
XLA Ops:
  0.6 117.9 %block.1 = (bf16[8,64,768]{2,1,0:T(8,128)(2,1)}, bf16[8,64,768]{2,1,0:T(8,128)(2,1)}, bf16[512,1024]{1,0:T(8,128)(2,1)}, bf16[512,1024]{1,0:T(8,128)(2,1)}) custom-call(bf16[512,768]{1,0:T(8,128)(2,1)} %resid.1, bf16[512,768]{1,0:T(8,128)(2,1)} %attn.1, bf16[512,768]{1,0:T(8,128)(2,1)} %attn_tan.1, s32[512,768]{1,0:T(8,128)} %probe.1, f32[768]{0:T(1024)} %gain.1, ...), custom_call_target="tpu_custom_call" | custom-call | tf_op jit(solution)/shard_map/block/pallas_call | solution.py:501
  118.5 3.1 %settle.1 = (bf16[8,64,768]{2,1,0:T(8,128)(2,1)}, bf16[8,64,768]{2,1,0:T(8,128)(2,1)}, bf16[512,1024]{1,0:T(8,128)(2,1)}, bf16[512,1024]{1,0:T(8,128)(2,1)}) custom-call(bf16[8,64,768]{2,1,0:T(8,128)(2,1)} %get-tuple-element.12.refs_0_, bf16[8,64,768]{2,1,0:T(8,128)(2,1)} %get-tuple-element.13.refs_1_, bf16[512,1024]{1,0:T(8,128)(2,1)} %get-tuple-element.14.refs_2_, ...), custom_call_target="tpu_custom_call" | custom-call | tf_op jit(solution)/shard_map/settle/pallas_call | solution.py:536

commit v6 on v5

--- a/solution.py
+++ b/solution.py
@@ -340,8 +340,8 @@
         (dict(z_near=3), ((near_pair, 3, (0, 2, 6)),)),
         (dict(sibling=5), ((whole, 0, (5,)), (whole, 1, (5,)))),
         (dict(), ((near, 2, (5,)), (near_pair, 3, (4,)))),
-        (dict(z_far=2), ((far, 2, (4, 6)),)),
-        (dict(z_far=3), ((far, 3, (4, 6)), (far, 2, (0, 2)), (far, 3, (0, 2)))),
+        (dict(z_far=2), ((far, 2, (4, 6, 0)),)),
+        (dict(z_far=3), ((far, 3, (4, 6)), (far, 2, (2,)), (far, 3, (0, 2)))),
     )
     slots = [sum((e.get(k, -1) + 1) << 4 * n for n, k in enumerate(kinds)) for e, _ in plan]
     items = [[how << 5 | j << 3 | i for how, j, steps in todo for i in steps] for _, todo in plan]
@@ -475,16 +475,13 @@
 
 def settle(*refs):
     ins, outs, held, sems = refs[:4], refs[4:8], refs[8:12], refs[12]
-    pieces = []
-    for n in range(4):
-        for half in range(2):
-            size = ins[n].shape[0] // 2
-            rows = pl.ds(half * size, size)
-            k = 2 * n + half
-            pieces.append((
-                pltpu.make_async_copy(ins[n].at[rows], held[n].at[rows], sems.at[0, k]),
-                pltpu.make_async_copy(held[n].at[rows], outs[n].at[rows], sems.at[1, k]),
-            ))
+    pieces = [
+        (
+            pltpu.make_async_copy(ins[n], held[n], sems.at[0, n]),
+            pltpu.make_async_copy(held[n], outs[n], sems.at[1, n]),
+        )
+        for n in range(4)
+    ]
     for get, _ in pieces:
         get.start()
     for get, put in pieces:
@@ -539,7 +536,7 @@
         out_shape=tuple(jax.ShapeDtypeStruct(a.shape, a.dtype) for a in found),
         in_specs=[hbm] * 4,
         out_specs=(hbm,) * 4,
-        scratch_shapes=[*(pltpu.VMEM(a.shape, a.dtype) for a in found), dma((2, 8))],
+        scratch_shapes=[*(pltpu.VMEM(a.shape, a.dtype) for a in found), dma((2, 4))],
         compiler_params=pltpu.CompilerParams(vmem_limit_bytes=62 << 20),
     )(*found)
     return state.reshape(TOK, FEAT), state_tan.reshape(TOK, FEAT), hidden, hidden_tan

time: 123 us -> 123 us (level)
  no operation moved by 1% of the time
where the time goes in v6:
time: 123 us; the launch traced here: 122 us
  Pallas kernels  121 us (98%)
    pallas_call x1, Pallas kernels, local(): pl.pallas_call(body, name='block', out_shape=(jax.ShapeDtypeStruct((TOK /...  118 us
    pallas_call x1, Pallas kernels, local(): pl.pallas_call(settle, name='settle', out_shape=tuple((jax.ShapeDtypeStru...  3.09 us

profile of v6, /device:TPU:1, one launch (start us, length us, event | category | flops | bytes accessed | tf_op | source)
XLA Modules:
  0.0 121.6 jit_solution(2340040127042645348)
XLA Ops:
  0.6 117.9 %block.1 = (bf16[8,64,768]{2,1,0:T(8,128)(2,1)}, bf16[8,64,768]{2,1,0:T(8,128)(2,1)}, bf16[512,1024]{1,0:T(8,128)(2,1)}, bf16[512,1024]{1,0:T(8,128)(2,1)}) custom-call(bf16[512,768]{1,0:T(8,128)(2,1)} %resid.1, bf16[512,768]{1,0:T(8,128)(2,1)} %attn.1, bf16[512,768]{1,0:T(8,128)(2,1)} %attn_tan.1, s32[512,768]{1,0:T(8,128)} %probe.1, f32[768]{0:T(1024)} %gain.1, ...), custom_call_target="tpu_custom_call" | custom-call | tf_op jit(solution)/shard_map/block/pallas_call | solution.py:498
  118.5 3.1 %settle.1 = (bf16[8,64,768]{2,1,0:T(8,128)(2,1)}, bf16[8,64,768]{2,1,0:T(8,128)(2,1)}, bf16[512,1024]{1,0:T(8,128)(2,1)}, bf16[512,1024]{1,0:T(8,128)(2,1)}) custom-call(bf16[8,64,768]{2,1,0:T(8,128)(2,1)} %get-tuple-element.12.refs_0_, bf16[8,64,768]{2,1,0:T(8,128)(2,1)} %get-tuple-element.13.refs_1_, bf16[512,1024]{1,0:T(8,128)(2,1)} %get-tuple-element.14.refs_2_, ...), custom_call_target="tpu_custom_call" | custom-call | tf_op jit(solution)/shard_map/settle/pallas_call | solution.py:533
